TPU v7x, 32 devices: a whole 2x2x4 slice. The times are simulated.
32 devices in a mesh: row: 2 (over y), col: 16 (over z, x, core).
Axes of the slice: x: 2, y: 2, z: 4, core: 2. Of those that a mesh axis runs over, the one named last changes fastest.
Arguments:
- region: bfloat16 [32, 768, 96], P('row', 'col'), may hold values from -6 to 6
- cotangent: bfloat16 [32, 768, 96], P('row', 'col'), may hold values from -6 to 6
- norm_gains: float32 [2, 2, 96], replicated, may hold values from 0.5 to 1.5
- qkv_weight: bfloat16 [2, 96, 288], replicated, may hold values from -0.625 to 0.625
- qkv_bias: float32 [2, 288], replicated, may hold values from -3 to 3
- bias_table: float32 [2, 3, 225], replicated, may hold values from -4 to 300
- proj_weight: bfloat16 [2, 96, 96], replicated, may hold values from -0.625 to 0.625
- up_weight: bfloat16 [2, 96, 384], replicated, may hold values from -0.625 to 0.625
- up_bias: float32 [2, 384], replicated, may hold values from -3 to 3
- down_weight: bfloat16 [2, 384, 96], replicated, may hold values from -0.3125 to 0.3125
Outputs:
- output: bfloat16 [32, 768, 96], P('row', 'col')
- grad_region: float32 [32, 768, 96], P('row', 'col')
- grad_gains: float32 [2, 2, 96], replicated
- grad_qkv_weight: float32 [2, 96, 288], replicated
- grad_qkv_bias: float32 [2, 288], replicated
- grad_table: float32 [2, 3, 225], replicated
- grad_proj: float32 [2, 96, 96], replicated
- grad_up_weight: float32 [2, 96, 384], replicated
- grad_up_bias: float32 [2, 384], replicated
- grad_down_weight: float32 [2, 384, 96], replicated
All inputs are finite; a program needn't handle non-finite values.
Results may differ from a plain program's by a relative error of at most 0.025.
Values may be sent and summed in bfloat16 or wider, within the bound.
A program may use at most 64 MiB of HBM per device.

v0:
```python
import jax
import jax.numpy as jnp
from jax import lax
from jax.sharding import PartitionSpec as P

WIN = 8


HIGHEST = lax.Precision.HIGHEST


def padded_2(shard, sides, width):
    for axis, dim in sides:
        count, length = (lax.axis_size(axis), shard.shape[dim])
        up = [(i, (i + 1) % count) for i in range(count - 1)]
        down = [(j, i) for i, j in up]
        last = lax.slice_in_dim(shard, length - width, length, axis=dim)
        initial = lax.slice_in_dim(shard, 0, width, axis=dim)
        before = lax.ppermute(last, axis, up)
        after = lax.ppermute(initial, axis, down)
        shard = jnp.concatenate([before, shard, after], axis=dim)
    return shard


def for_sending(shard):
    return jax.tree.map(lambda a: a.astype(jnp.bfloat16) if a.dtype == jnp.float32 else a, shard)


def layer_norm(values, gain):
    average = jnp.mean(values, -1, keepdims=True)
    centred = values - average
    variance = jnp.mean(centred * centred, -1, keepdims=True)
    return centred * lax.rsqrt(variance + 1e-05) * gain


def position_bias(table):
    positions = jnp.arange(WIN * WIN, dtype=jnp.int32)
    pos_row = positions // WIN
    pos_col = positions % WIN
    table_side = 2 * WIN - 1
    table_index = (pos_row[:, None] - pos_row[None, :] + WIN - 1) * table_side + (
        pos_col[:, None] - pos_col[None, :] + WIN - 1
    )
    onehot = (
        table_index[:, :, None]
        == jnp.arange(table_side * table_side, dtype=jnp.int32)[None, None, :]
    ).astype(jnp.float32)
    return jnp.einsum("qkt,ht->hqk", onehot, table, precision=HIGHEST)


def windowize(field):
    height, width, depth = field.shape
    blocks = field.reshape(height // WIN, WIN, width // WIN, WIN, depth)
    return blocks.transpose(0, 2, 1, 3, 4).reshape(-1, WIN * WIN, depth)


def unwindowize(windows, height, width):
    depth = windows.shape[-1]
    blocks = windows.reshape(height // WIN, width // WIN, WIN, WIN, depth)
    return blocks.transpose(0, 2, 1, 3, 4).reshape(height, width, depth)


def attend(windows, usable, layer):
    gain_pair, qkv_weight, qkv_bias, table, proj_weight = layer[:5]
    win_count, win_tokens, channels = windows.shape
    head_count = table.shape[0]
    head_size = channels // head_count
    normed = (
        layer_norm(windows, gain_pair[0])
        .astype(jnp.bfloat16)
        .reshape(win_count * win_tokens, channels)
    )
    triple = (jnp.dot(normed, qkv_weight, preferred_element_type=jnp.float32) + qkv_bias).astype(
        jnp.bfloat16
    )
    triple = triple.reshape(win_count, win_tokens, 3, head_count, head_size)
    queries = triple[:, :, 0]
    key_part = triple[:, :, 1]
    value_part = triple[:, :, 2]
    scores = (
        jnp.einsum("wqhd,wkhd->whqk", queries, key_part, preferred_element_type=jnp.float32)
        * head_size ** (-0.5)
        + position_bias(table)[None]
    )
    if usable is not None:
        scores = jnp.where(usable[:, None, None, :], scores, -1e30)
    highest = lax.stop_gradient(jnp.max(scores, -1, keepdims=True))
    exponent = jnp.exp(scores - highest)
    softmax_w = (exponent / jnp.sum(exponent, -1, keepdims=True)).astype(jnp.bfloat16)
    mixture = jnp.einsum(
        "whqk,wkhd->wqhd", softmax_w, value_part, preferred_element_type=jnp.float32
    ).astype(jnp.bfloat16)
    mixture = mixture.reshape(win_count * win_tokens, channels)
    projected = jnp.dot(mixture, proj_weight, preferred_element_type=jnp.float32)
    return windows + projected.reshape(win_count, win_tokens, channels)


def feed(field, layer):
    gain_pair = layer[0]
    up_weight, up_bias, down_weight = layer[5:]
    channels = field.shape[-1]
    flat_rows = field.reshape(-1, channels)
    normed = layer_norm(flat_rows, gain_pair[1]).astype(jnp.bfloat16)
    hidden = jax.nn.gelu(
        jnp.dot(normed, up_weight, preferred_element_type=jnp.float32) + up_bias
    ).astype(jnp.bfloat16)
    return (flat_rows + jnp.dot(hidden, down_weight, preferred_element_type=jnp.float32)).reshape(
        field.shape
    )


def regular(field, layer):
    height, width, _ = field.shape
    return feed(unwindowize(attend(windowize(field), None, layer), height, width), layer)


def shifted(padded, row_start, col_start, total_rows, total_cols, layer):
    half_win = WIN // 2
    height = padded.shape[0] - WIN
    width = padded.shape[1] - WIN
    row_ids = row_start + jnp.arange(height + WIN, dtype=jnp.int32)
    col_ids = col_start + jnp.arange(width + WIN, dtype=jnp.int32)
    inside = ((row_ids >= 0) & (row_ids < total_rows))[:, None] & (
        (col_ids >= 0) & (col_ids < total_cols)
    )[None, :]
    usable = windowize(inside[:, :, None]).reshape(-1, WIN * WIN)
    mixed_field = unwindowize(attend(windowize(padded), usable, layer), height + WIN, width + WIN)
    return feed(mixed_field[half_win : half_win + height, half_win : half_win + width], layer)


def edge_strips(gradient, dim):
    half_win = WIN // 2
    length = gradient.shape[dim]
    head_strip = lax.slice_in_dim(gradient, 0, half_win, axis=dim)
    tail_strip = lax.slice_in_dim(gradient, length - half_win, length, axis=dim)
    return jnp.concatenate([head_strip, tail_strip], dim)


def fold_edges(gradient, widened, dim):
    half_win = WIN // 2
    length = gradient.shape[dim]
    interior = lax.slice_in_dim(gradient, half_win, length - half_win, axis=dim)
    from_lower = lax.slice_in_dim(widened, 0, half_win, axis=dim)
    from_upper = lax.slice_in_dim(widened, 3 * half_win, 4 * half_win, axis=dim)
    inner_len = length - 2 * half_win
    widths_low = [(0, 0)] * gradient.ndim
    widths_low[dim] = (0, inner_len - half_win)
    widths_high = [(0, 0)] * gradient.ndim
    widths_high[dim] = (inner_len - half_win, 0)
    return interior + jnp.pad(from_lower, widths_low) + jnp.pad(from_upper, widths_high)


def flatten(parts):
    return jnp.concatenate([part.astype(jnp.float32).reshape(-1) for part in parts])


def unflatten(flat_vec, shapes_like):
    pieces = []
    offset = 0
    for like in shapes_like:
        length = like.size
        pieces.append(flat_vec[offset : offset + length].reshape(like.shape))
        offset = offset + length
    return pieces


def body(
    region,
    cotangent,
    norm_gains,
    qkv_weight,
    qkv_bias,
    bias_table,
    proj_weight,
    up_weight,
    up_bias,
    down_weight,
):
    stacked = (
        norm_gains,
        qkv_weight,
        qkv_bias,
        bias_table,
        proj_weight,
        up_weight,
        up_bias,
        down_weight,
    )
    lower_layer = tuple((entry[0] for entry in stacked))
    upper_layer = tuple((entry[1] for entry in stacked))
    half_win = WIN // 2
    tile_rows, tile_cols, channels = region.shape
    total_rows = tile_rows * lax.axis_size("row")
    total_cols = tile_cols * lax.axis_size("col")
    row_start = lax.axis_index("row") * tile_rows - half_win
    col_start = lax.axis_index("col") * tile_cols - half_win
    lower_out, pull_lower = jax.vjp(regular, region.astype(jnp.float32), lower_layer)
    lower_bf = lower_out.astype(jnp.bfloat16)
    padded = padded_2(lower_bf, (("row", 0), ("col", 1)), half_win)

    def upper_block(field, layer):
        return shifted(field, row_start, col_start, total_rows, total_cols, layer)

    upper_out, pull_upper = jax.vjp(upper_block, padded.astype(jnp.float32), upper_layer)
    grad_padded, grad_upper = pull_upper(cotangent.astype(jnp.float32))
    upper_flat = flatten(grad_upper)
    widened = padded_2(
        edge_strips(grad_padded, 1).astype(jnp.bfloat16), (("col", 1),), half_win
    ).astype(jnp.float32)
    partial_grad = fold_edges(grad_padded, widened, 1)
    widened = padded_2(for_sending(edge_strips(partial_grad, 0)), (("row", 0),), half_win)
    grad_lower = fold_edges(partial_grad, widened, 0)
    grad_region, grad_lower_layer = pull_lower(grad_lower)
    lower_flat = flatten(grad_lower_layer)
    lower_total, upper_total = lax.psum((lower_flat, upper_flat), ("row", "col"))
    lower_parts = unflatten(lower_total, lower_layer)
    upper_parts = unflatten(upper_total, upper_layer)
    grads = [jnp.stack([low_part, up_part]) for low_part, up_part in zip(lower_parts, upper_parts)]
    return (
        upper_out.astype(jnp.bfloat16),
        grad_region,
        grads[0],
        grads[1],
        grads[2],
        grads[3],
        grads[4],
        grads[5],
        grads[6],
        grads[7],
    )


def solution(mesh):
    return jax.shard_map(
        body,
        mesh=mesh,
        in_specs=(
            P("row", "col", None),
            P("row", "col", None),
            P(),
            P(),
            P(),
            P(),
            P(),
            P(),
            P(),
            P(),
        ),
        out_specs=(
            P("row", "col", None),
            P("row", "col", None),
            P(),
            P(),
            P(),
            P(),
            P(),
            P(),
            P(),
            P(),
        ),
        check_vma=False,
    )
```

profile of v0, /device:TPU:0, one launch (start us, length us, event | category | flops | bytes accessed | tf_op | source)
XLA Modules:
  0.0 316.9 jit_solution(1001356604226127183)
XLA Ops:
  10.1 1.4 slice_reduce_fusion.1
  13.7 2.8 fusion.69
  25.9 4.9 %collective-permute-start = (bf16[4,48,96]{2,1,0:T(8,128)(2,1)S(1)}, bf16[4,48,96]{2,1,0:T(8,128)(2,1)S(1)}, u32[]{:S(2)}, u32[]{:S(2)}) collective-permute-start(bf16[4,48,96]{2,1,0:T(8,128)(2,1)S(1)} %bitcast.372), channel_id=1, source_target_pairs={{0,16},{1,17},{2,18},{3,19},{4,20},{5,21},{6,22},{7,23},{8,24},{9,... | collective-permute-start | bytes 110600 | tf_op jit(solution)/shard_map/ppermute | solution.py:19
  31.5 2.8 fusion.70
  34.5 1.5 collective-permute-start.2
  47.3 1.5 reshape.734
  50.2 2.4 fusion.184
  53.2 1.5 convolution_convert_fusion.7
  58.0 2.0 multiply_convert_fusion.3
  61.6 2.4 fusion.185
  65.2 2.5 fusion.65
  73.7 2.2 reshape.743
  75.9 1.8 fusion.32
  83.3 13.9 %reshape.744 = bf16[1344,288]{0,1:T(8,128)(2,1)S(1)} reshape(bf16[21,64,3,3,32]{1,0,4,3,2:T(8,128)(2,1)S(1)} %copy.219) | data formatting | bytes 1548288 | tf_op jit(solution)/shard_map/transpose(jvp())/reshape | solution.py:76
  97.2 2.1 fusion.74
  106.2 1.8 fusion.77
  112.6 5.7 %collective-permute-start.4 = (bf16[24,4,96]{2,1,0:T(4,128)(2,1)S(1)}, bf16[24,4,96]{2,1,0:T(4,128)(2,1)S(1)}, u32[]{:S(2)}, u32[]{:S(2)}) collective-permute-start(bf16[24,4,96]{2,1,0:T(4,128)(2,1)S(1)} %get-tuple-element.82), channel_id=1, source_target_pairs={{0,1},{1,2},{2,3},{3,4},{4,5},{5,6},{6,7},{7,8},{8,9},{9,10},{10,1... | collective-permute-start | bytes 55304 | tf_op jit(solution)/shard_map/ppermute | solution.py:19
  119.6 1.4 fusion.82
  121.1 1.6 collective-permute-done.5
  122.9 2.4 collective-permute-start.6
  128.3 7.7 %concatenate.24 = f32[112131]{0:T(1024)} concatenate(f32[192]{0:T(256)S(1)} %reshape.767, f32[27648]{0:T(1024)S(1)} %reshape.789, f32[288]{0:T(512)S(1)} %reduce_sum.330, f32[675]{0:T(1024)S(1)} %reshape.770, f32[9216]{0:T(1024)S(1)} %reshape.791, f32[36864]{0:T(1024)S(1)} %reshape.793, f32[384]{0:T(512)S(1)} %copy-done.84, f32[36864]{0:T(1024)S(1)} %reshape.795), dimensions={0} | concatenate | bytes 897048 | tf_op jit(solution)/shard_map/concatenate | solution.py:154
  148.2 1.4 fusion.81
  150.1 7.8 %concatenate.23 = f32[112131]{0:T(1024)} concatenate(f32[192]{0:T(256)S(1)} %reshape.755, f32[27648]{0:T(1024)S(1)} %reshape.781, f32[288]{0:T(512)S(1)} %reduce_sum.321, f32[675]{0:T(1024)S(1)} %reshape.758, f32[9216]{0:T(1024)S(1)} %reshape.783, f32[36864]{0:T(1024)S(1)} %reshape.785, f32[384]{0:T(512)S(1)} %get-tuple-element.128, f32[36864]{0:T(1024)S(1)} %reshape.787), dimensions={0} | concatenate | bytes 897048 | tf_op jit(solution)/shard_map/concatenate | solution.py:154
  159.4 133.2 %all-reduce.18.cloned.1.call-done = (f32[112131]{0:T(1024)}, f32[112131]{0:T(1024)}) async-done(((f32[112131]{0:T(1024)}, f32[112131]{0:T(1024)}), (f32[112131]{0:T(1024)}, f32[112131]{0:T(1024)})) %all-reduce.18.cloned.1.call-update) | async-done | bytes 897064 | tf_op jit(solution)/shard_map/psum | solution.py:215
  (405 shorter events, 92.2 us)
Async XLA Ops:
  7.2 285.4 %all-reduce.18.cloned.1.call-start = ((), (), s32[]{:S(2)}) async-start(), calls=%async_computation | async-start | bytes 1802240 | tf_op jit(solution)/shard_map/psum | solution.py:215
  9.3 7.3 %copy-start = (bf16[16,48,96]{2,1,0:T(8,128)(2,1)S(1)}, bf16[16,48,96]{2,1,0:T(8,128)(2,1)}, u32[]{:S(2)}) copy-start(bf16[16,48,96]{2,1,0:T(8,128)(2,1)} %param.10) | copy-start | bytes 442372
  10.1 6.8 %copy-start.77 = (f32[96]{0:T(128)}, f32[96]{0:T(128)S(1)}, u32[]{:S(2)}) copy-start(f32[96]{0:T(128)S(1)} %get-tuple-element.112) | copy-start | bytes 1156
  10.1 34.6 %copy-start.74 = (f32[96]{0:T(128)}, f32[96]{0:T(128)S(1)}, u32[]{:S(2)}) copy-start(f32[96]{0:T(128)S(1)} %get-tuple-element.113) | copy-start | bytes 1156
  12.2 25.2 %copy-start.11 = (f32[2,6,8,8]{3,1,2,0:T(8,128)}, f32[2,6,8,8]{3,1,2,0:T(8,128)S(1)}, u32[]{:S(2)}) copy-start(f32[2,6,8,8]{3,1,2,0:T(8,128)S(1)} %broadcast_multiply_fusion.2) | copy-start | bytes 9220
  13.7 17.8 %copy-start.69 = (s32[64,64]{1,0:T(8,128)}, s32[64,64]{1,0:T(8,128)S(1)}, u32[]{:S(2)}) copy-start(s32[64,64]{1,0:T(8,128)S(1)} %add_add_fusion.8) | copy-start | bytes 49156
  24.5 9.9 %collective-permute-start.1 = (bf16[4,48,96]{2,1,0:T(8,128)(2,1)S(1)}, bf16[4,48,96]{2,1,0:T(8,128)(2,1)S(1)}, u32[]{:S(2)}, u32[]{:S(2)}) collective-permute-start(bf16[4,48,96]{2,1,0:T(8,128)(2,1)S(1)} %bitcast.371), channel_id=1, source_target_pairs={{16,0},{17,1},{18,2},{19,3},{20,4},{21,5},{22,6},{23,7},{24,8},{25... | collective-permute-start | bytes 110600 | tf_op jit(solution)/shard_map/ppermute | solution.py:20
  25.9 8.5 %collective-permute-start = (bf16[4,48,96]{2,1,0:T(8,128)(2,1)S(1)}, bf16[4,48,96]{2,1,0:T(8,128)(2,1)S(1)}, u32[]{:S(2)}, u32[]{:S(2)}) collective-permute-start(bf16[4,48,96]{2,1,0:T(8,128)(2,1)S(1)} %bitcast.372), channel_id=1, source_target_pairs={{0,16},{1,17},{2,18},{3,19},{4,20},{5,21},{6,22},{7,23},{8,24},{9,... | collective-permute-start | bytes 110600 | tf_op jit(solution)/shard_map/ppermute | solution.py:19
  31.4 8.2 %copy-start.58 = (bf16[16,48,96]{2,1,0:T(8,128)(2,1)S(1)}, bf16[16,48,96]{2,1,0:T(8,128)(2,1)}, u32[]{:S(2)}) copy-start(bf16[16,48,96]{2,1,0:T(8,128)(2,1)} %param.11) | copy-start | bytes 442372
  34.5 8.5 %collective-permute-start.2 = (bf16[24,4,96]{2,1,0:T(4,128)(2,1)S(1)}, bf16[24,4,96]{2,1,0:T(4,128)(2,1)S(1)}, u32[]{:S(2)}, u32[]{:S(2)}) collective-permute-start(bf16[24,4,96]{2,1,0:T(4,128)(2,1)S(1)} %get-tuple-element.86), channel_id=1, source_target_pairs={{0,1},{1,2},{2,3},{3,4},{4,5},{5,6},{6,7},{7,8},{8,9},{9,10},{10,1... | collective-permute-start | bytes 55304 | tf_op jit(solution)/shard_map/ppermute | solution.py:19
  36.0 7.0 %collective-permute-start.3 = (bf16[24,4,96]{2,1,0:T(4,128)(2,1)S(1)}, bf16[24,4,96]{2,1,0:T(4,128)(2,1)S(1)}, u32[]{:S(2)}, u32[]{:S(2)}) collective-permute-start(bf16[24,4,96]{2,1,0:T(4,128)(2,1)S(1)} %get-tuple-element.87), channel_id=1, source_target_pairs={{1,0},{2,1},{3,2},{4,3},{5,4},{6,5},{7,6},{8,7},{9,8},{10,9},{11,1... | collective-permute-start | bytes 55304 | tf_op jit(solution)/shard_map/ppermute | solution.py:20
  111.6 8.0 %copy-start.70 = (s32[64,64]{1,0:T(8,128)S(1)}, s32[64,64]{1,0:T(8,128)}, u32[]{:S(2)}) copy-start(s32[64,64]{1,0:T(8,128)} %copy-done.69) | copy-start | bytes 49156
  112.6 8.5 %collective-permute-start.4 = (bf16[24,4,96]{2,1,0:T(4,128)(2,1)S(1)}, bf16[24,4,96]{2,1,0:T(4,128)(2,1)S(1)}, u32[]{:S(2)}, u32[]{:S(2)}) collective-permute-start(bf16[24,4,96]{2,1,0:T(4,128)(2,1)S(1)} %get-tuple-element.82), channel_id=1, source_target_pairs={{0,1},{1,2},{2,3},{3,4},{4,5},{5,6},{6,7},{7,8},{8,9},{9,10},{10,1... | collective-permute-start | bytes 55304 | tf_op jit(solution)/shard_map/ppermute | solution.py:19
  118.3 4.3 %collective-permute-start.5 = (bf16[24,4,96]{2,1,0:T(4,128)(2,1)S(1)}, bf16[24,4,96]{2,1,0:T(4,128)(2,1)S(1)}, u32[]{:S(2)}, u32[]{:S(2)}) collective-permute-start(bf16[24,4,96]{2,1,0:T(4,128)(2,1)S(1)} %get-tuple-element.83), channel_id=1, source_target_pairs={{1,0},{2,1},{3,2},{4,3},{5,4},{6,5},{7,6},{8,7},{9,8},{10,9},{11,1... | collective-permute-start | bytes 55304 | tf_op jit(solution)/shard_map/ppermute | solution.py:20
  121.0 5.6 %copy-start.85 = (f32[96]{0:T(128)S(1)}, f32[96]{0:T(128)}, u32[]{:S(2)}) copy-start(f32[96]{0:T(128)} %get-tuple-element.56) | copy-start | bytes 1156
  121.1 5.6 %copy-start.86 = (f32[96]{0:T(128)S(1)}, f32[96]{0:T(128)}, u32[]{:S(2)}) copy-start(f32[96]{0:T(128)} %get-tuple-element.50) | copy-start | bytes 1156
  121.1 5.6 %copy-start.65 = (f32[384,96]{0,1:T(8,128)S(1)}, f32[384,96]{0,1:T(8,128)}, u32[]{:S(2)}) copy-start(f32[384,96]{0,1:T(8,128)} %fusion.73) | copy-start | bytes 442372
  122.9 5.4 %copy-start.84 = (f32[384]{0:T(512)S(1)}, f32[384]{0:T(512)}, u32[]{:S(2)}) copy-start(f32[384]{0:T(512)} %get-tuple-element.126) | copy-start | bytes 4612
  122.9 13.1 %collective-permute-start.6 = (bf16[4,48,96]{2,1,0:T(8,128)(2,1)S(1)}, bf16[4,48,96]{2,1,0:T(8,128)(2,1)S(1)}, u32[]{:S(2)}, u32[]{:S(2)}) collective-permute-start(bf16[4,48,96]{2,1,0:T(8,128)(2,1)S(1)} %get-tuple-element.84), channel_id=1, source_target_pairs={{0,16},{1,17},{2,18},{3,19},{4,20},{5,21},{6,22},{7,23},{8,24},{9,... | collective-permute-start | bytes 110600 | tf_op jit(solution)/shard_map/ppermute | solution.py:19
  125.3 10.7 %collective-permute-start.7 = (bf16[4,48,96]{2,1,0:T(8,128)(2,1)S(1)}, bf16[4,48,96]{2,1,0:T(8,128)(2,1)S(1)}, u32[]{:S(2)}, u32[]{:S(2)}) collective-permute-start(bf16[4,48,96]{2,1,0:T(8,128)(2,1)S(1)} %get-tuple-element.85), channel_id=1, source_target_pairs={{16,0},{17,1},{18,2},{19,3},{20,4},{21,5},{22,6},{23,7},{24,8},{25... | collective-permute-start | bytes 110600 | tf_op jit(solution)/shard_map/ppermute | solution.py:20
  127.8 8.3 %copy-start.24 = (f32[768,384]{1,0:T(8,128)S(1)}, f32[768,384]{1,0:T(8,128)}, u32[]{:S(2)}) copy-start(f32[768,384]{1,0:T(8,128)} %copy-done.23) | copy-start | bytes 3538948
  149.6 8.3 %copy-start.26 = (f32[768,96]{0,1:T(8,128)S(1)}, f32[768,96]{0,1:T(8,128)}, u32[]{:S(2)}) copy-start(f32[768,96]{0,1:T(8,128)} %copy.243) | copy-start | bytes 884740
  149.6 8.3 %copy-start.72 = (f32[768]{0:T(1024)S(1)}, f32[768]{0:T(1024)}, u32[]{:S(2)}) copy-start(f32[768]{0:T(1024)} %div.191) | copy-start | bytes 9220
  292.6 10.8 %copy-start.46 = (f32[112131]{0:T(1024)S(1)}, f32[112131]{0:T(1024)}, u32[]{:S(2)}) copy-start(f32[112131]{0:T(1024)} %get-tuple-element.63) | copy-start | bytes 1345576
  (75 other events, 132.9 us)
Sparse Core Ops, SparseCore 0:
  158.0 134.4 all-reduce.17
where the time goes:
time: 319 us; the launch traced here: 317 us
  waiting for transfers between devices  135 us (42%)
  local copies, waits for them, and re-layouts  84.4 us (26%)
  matrix products  37 us (12%)
  other arithmetic  25.1 us (8%)
  starting transfers between devices  19.7 us (6%)
  between operations  16 us (5%)
    psum x1, waiting for transfers between devices, body(): lax.psum((lower_flat, upper_flat), ('row', 'col'))  133 us
    reshape x4, local copies, waits for them, and re-layouts, attend(): triple = triple.reshape(win_count, win_tokens, 3, head_count, head_size)  16.9 us
    concatenate x2, local copies, waits for them, and re-layouts, flatten(): jnp.concatenate([part.astype(jnp.float32).reshape(-1) for part in parts])  15.5 us
    ppermute x4, starting transfers between devices, padded_2(): before = lax.ppermute(last, axis, up)  14.5 us
    unnamed x182, local copies, waits for them, and re-layouts  11 us
    slice x14, local copies, waits for them, and re-layouts, unflatten(): pieces.append(flat_vec[offset:offset + length].reshape(like.shape))  10.9 us
    dot_general x4, matrix products, position_bias(): return jnp.einsum('qkt,ht->hqk', onehot, table, precision=HIGHEST)  8.48 us
    dot_general x6, matrix products, feed(): jnp.dot(hidden, down_weight, preferred_element_type=jnp.float32)  8.12 us
  transfers between devices with their start and end apart: 9, of which 2 were waited for; matrix products, arithmetic and copies ran while one was open for 7% of the time, Pallas kernels for 0%

commit v1 on v0

v1 whole, which is shorter than its diff:
```python
import functools

import jax
import jax.numpy as jnp
from jax import lax
from jax.experimental import pallas as pl
from jax.experimental.pallas import tpu as pltpu
from jax.sharding import PartitionSpec as P

WIN = 8
HALF = 4
TOK = 64
BF = jnp.bfloat16
F32 = jnp.float32
MESH = pl.DeviceIdType.MESH

U_QKV = 0
U_PROJ = 18
U_UP = 24
U_DOWN = 42
U_SMALL = 60
U_BLOCK = 62


def dot_nn(a, b):
    return lax.dot_general(a, b, (((1,), (0,)), ((), ())), preferred_element_type=F32)


def dot_nt(a, b):
    return lax.dot_general(a, b, (((1,), (1,)), ((), ())), preferred_element_type=F32)


def dot_tn(a, b):
    return lax.dot_general(a, b, (((0,), (0,)), ((), ())), preferred_element_type=F32)


def norm(x):
    average = jnp.mean(x, -1, keepdims=True)
    centred = x - average
    rstd = lax.rsqrt(jnp.mean(centred * centred, -1, keepdims=True) + 1e-05)
    return centred * rstd, rstd


def norm_back(dy, gain, xhat, rstd):
    dx = dy * gain
    return rstd * (
        dx - jnp.mean(dx, -1, keepdims=True) - xhat * jnp.mean(dx * xhat, -1, keepdims=True)
    )


def seg_first(shape):
    return lax.broadcasted_iota(jnp.int32, shape, 1) < TOK


def seg_reduce(fn, fill, s):
    lo, hi = s[:, :128], s[:, 128:]
    first = seg_first(lo.shape)
    r0 = fn(jnp.where(first, lo, fill), -1, keepdims=True)
    r1 = fn(jnp.where(first, fill, lo), -1, keepdims=True)
    r2 = fn(hi, -1, keepdims=True)
    return r0, r1, r2


def seg_spread(parts, like):
    r0, r1, r2 = parts
    lo = jnp.where(seg_first((like.shape[0], 128)), r0, r1)
    hi = jnp.broadcast_to(r2, (like.shape[0], 64))
    return jnp.concatenate([lo, hi], 1)


def softmax(s):
    e = jnp.exp(s - seg_spread(seg_reduce(jnp.max, -jnp.inf, s), s))
    sums = seg_reduce(jnp.sum, 0.0, e)
    return e * seg_spread(tuple(1.0 / t for t in sums), s)


def head_masks(channels):
    lane = lax.broadcasted_iota(jnp.int32, (1, channels), 1)
    size = channels // 3
    return [((lane >= h * size) & (lane < (h + 1) * size)) for h in range(3)]


def stack_heads(x, masks):
    zero = jnp.zeros_like(x)
    return jnp.concatenate([jnp.where(m, x, zero) for m in masks], 0)


def fold_heads(x, masks):
    out = jnp.where(masks[0], x[:TOK], 0.0)
    for h in (1, 2):
        out = out + jnp.where(masks[h], x[h * TOK : (h + 1) * TOK], 0.0)
    return out


def factors(n_row, n_col):
    phases = [[("col", 1, 2)], [("col", 2, 2), ("row", 1, n_row)], [("col", 4, n_col // 4)]]
    phases = [[f for f in p if f[2] > 1] for p in phases]
    return [p for p in phases if p]


def kernel(
    n_row,
    n_col,
    units,
    region,
    cot,
    gains,
    wqkv,
    bqkv,
    xtab,
    wproj,
    wup,
    bup,
    wdown,
    out,
    grad_region,
    o_qkv,
    o_proj,
    o_up,
    o_down,
    o_small,
    ws,
    bias,
    f0,
    h0,
    f1,
    h1,
    dh1,
    g1,
    a_qkv,
    a_proj,
    a_up,
    a_down,
    a_vec,
    a_bup,
    a_bias,
    hs_row,
    hr_row,
    hs_col,
    hr_col,
    halo_send,
    halo_recv,
    pack,
    *rest,
):
    rows, cols, channels = region.shape
    prow, pcol = rows + WIN, cols + WIN
    scale = (channels // 3) ** (-0.5)
    phases = factors(n_row, n_col)
    n_ph = len(phases)
    rs_recv = rest[:n_ph]
    rs_acc = rest[n_ph : 2 * n_ph]
    ag_buf = rest[2 * n_ph : 3 * n_ph]
    red_send, red_recv = rest[3 * n_ph :]
    index = {"row": lax.axis_index("row"), "col": lax.axis_index("col")}
    count = {"row": n_row, "col": n_col}

    def device(changes):
        where = dict(index)
        where.update(changes)
        return (where["row"], where["col"])

    def side(axis, step):
        n = count[axis]
        return device({axis: lax.rem(index[axis] + (step + n), n)})

    def members(phase):
        size = 1
        me = 0
        for _, stride, n in phase:
            size *= n
        partners = []
        digits = []
        for axis, stride, n in phase:
            digit = lax.rem(lax.div(index[axis], stride), n)
            digits.append(digit)
            me = me * n + digit
        for d in range(1, size):
            rest_d, ds = d, []
            for _, _, n in reversed(phase):
                ds.append(rest_d % n)
                rest_d //= n
            ds = ds[::-1]
            neg = 0
            member = 0
            changes = {}
            for (axis, stride, n), digit, step in zip(phase, digits, ds):
                neg = neg * n + (-step) % n
                other = lax.rem(digit + step, n)
                member = member * n + other
                changes[axis] = changes.get(axis, index[axis]) + (other - digit) * stride
            partners.append((d, neg, member, device(changes)))
        return size, me, partners

    groups = [members(p) for p in phases]

    barrier = pltpu.get_barrier_semaphore()
    greet = [side("col", -1), side("col", 1), side("row", -1), side("row", 1)]
    for _, _, partners in groups:
        greet += [p[3] for p in partners]
    for dev in greet:
        pl.semaphore_signal(barrier, inc=1, device_id=dev, device_id_type=MESH)

    for ref in (a_qkv, a_proj, a_up, a_down, a_vec, a_bup, a_bias, dh1, f1, pack):
        ref[...] = jnp.zeros(ref.shape, ref.dtype)
    for b in range(2):
        whole = wqkv[b].astype(F32)
        for t in range(3):
            ws[b, t] = whole[:, t * channels : (t + 1) * channels].astype(BF)
        for r in range(WIN):
            at = (WIN - 1 - r) * WIN
            bias[b, r * WIN : (r + 1) * WIN, :] = jnp.concatenate(
                [xtab[b, h][:, at : at + TOK] for h in range(3)], 1
            )
    f0[...] = region[...].astype(F32)
    masks = head_masks(channels)

    def qkv_of(u, b):
        xhat, rstd = norm(u)
        a = (xhat * gains[b, 0:1, :]).astype(BF)
        line = bqkv[b : b + 1, :]
        parts = [
            (dot_nn(a, ws[b, t]) + line[:, t * channels : (t + 1) * channels]).astype(BF)
            for t in range(3)
        ]
        return xhat, rstd, a, parts

    def window(q, k, v, b, usable):
        kbd, vbd = stack_heads(k, masks), stack_heads(v, masks)
        s = dot_nt(q, kbd) * scale + bias[b]
        if usable is not None:
            s = jnp.where(usable, s, -1e30)
        return kbd, vbd, softmax(s)

    def split(x, w):
        return x[w * TOK : (w + 1) * TOK]

    def attn_forward(u, b, usable):
        _, _, _, (q, k, v) = qkv_of(u, b)
        mixed = []
        for w in range(u.shape[0] // TOK):
            _, vbd, p = window(split(q, w), split(k, w), split(v, w), b, usable[w])
            mixed.append(dot_nn(p.astype(BF), vbd))
        mixed = jnp.concatenate(mixed, 0).astype(BF)
        return u + dot_nn(mixed, wproj[b])

    def attn_backward(u, dh, b, usable):
        xhat, rstd, a, (q, k, v) = qkv_of(u, b)
        dhb = dh.astype(BF)
        dmix = dot_nt(dhb, wproj[b]).astype(BF)
        mixed, dqs, dks, dvs = [], [], [], []
        dbias = None
        for w in range(u.shape[0] // TOK):
            qw, do = split(q, w), split(dmix, w)
            kbd, vbd, p = window(qw, split(k, w), split(v, w), b, usable[w])
            pb = p.astype(BF)
            mixed.append(dot_nn(pb, vbd))
            dp = dot_nt(do, vbd)
            ds = p * (dp - seg_spread(seg_reduce(jnp.sum, 0.0, dp * p), p))
            dbias = ds if dbias is None else dbias + ds
            dsb = (ds * scale).astype(BF)
            dqs.append(dot_nn(dsb, kbd))
            dks.append(fold_heads(dot_tn(dsb, qw), masks))
            dvs.append(fold_heads(dot_tn(pb, do), masks))
        mixed = jnp.concatenate(mixed, 0).astype(BF)
        a_proj[b] += dot_tn(mixed, dhb)
        a_bias[b] += dbias
        da = None
        for t, parts in enumerate((dqs, dks, dvs)):
            grad = jnp.concatenate(parts, 0)
            a_vec[b, t : t + 1, :] += jnp.sum(grad, 0, keepdims=True)
            grad = grad.astype(BF)
            a_qkv[b, t] += dot_tn(a, grad)
            term = dot_nt(grad, ws[b, t])
            da = term if da is None else da + term
        a_vec[b, 3:4, :] += jnp.sum(da * xhat, 0, keepdims=True)
        return dh + norm_back(da, gains[b, 0:1, :], xhat, rstd)

    def gelu(z):
        t = jnp.tanh(0.7978845608028654 * z * (1.0 + 0.044715 * z * z))
        return t, 0.5 * z * (1.0 + t)

    def feed_forward(h, b):
        xhat, _ = norm(h)
        f = (xhat * gains[b, 1:2, :]).astype(BF)
        _, m = gelu(dot_nn(f, wup[b]) + bup[b : b + 1, :])
        return h + dot_nn(m.astype(BF), wdown[b])

    def feed_backward(h, g, b, want_out):
        xhat, rstd = norm(h)
        f = (xhat * gains[b, 1:2, :]).astype(BF)
        z = dot_nn(f, wup[b]) + bup[b : b + 1, :]
        t, m = gelu(z)
        m = m.astype(BF)
        result = h + dot_nn(m, wdown[b]) if want_out else None
        gb = g.astype(BF)
        dm = dot_nt(gb, wdown[b])
        slope = 0.5 * (1.0 + t) + 0.5 * z * (1.0 - t * t) * (
            0.7978845608028654 * (1.0 + 0.134145 * z * z)
        )
        dz = dm * slope
        a_bup[b : b + 1, :] += jnp.sum(dz, 0, keepdims=True)
        dz = dz.astype(BF)
        a_down[b] += dot_tn(gb, m)
        a_up[b] += dot_tn(f, dz)
        df = dot_nt(dz, wup[b])
        a_vec[b, 4:5, :] += jnp.sum(df * xhat, 0, keepdims=True)
        return result, g + norm_back(df, gains[b, 1:2, :], xhat, rstd)

    def spots0(j):
        return [(i * WIN, pl.multiple_of((j * 2 + c) * WIN, WIN)) for i in range(rows // WIN) for c in range(2)]

    def spots1(j):
        return [(i * WIN, pl.multiple_of(j * WIN, WIN)) for i in range(prow // WIN)]

    def gather(ref, spots):
        return jnp.concatenate(
            [ref[r : r + WIN, pl.ds(c, WIN), :].reshape(TOK, channels) for r, c in spots], 0
        )

    def scatter(ref, spots, x):
        for w, (r, c) in enumerate(spots):
            ref[r : r + WIN, pl.ds(c, WIN), :] = split(x, w).reshape(WIN, WIN, channels)

    lane = lax.broadcasted_iota(jnp.int32, (1, 3 * TOK), 1)
    key_row = lax.div(lax.rem(lane, TOK), WIN)
    key_col = lax.rem(lane, WIN)

    def usable1(spots):
        found = []
        for r, c in spots:
            row = key_row + (index["row"] * rows - HALF + r)
            col = key_col + (index["col"] * cols - HALF + c)
            found.append(
                (row >= 0) & (row < n_row * rows) & (col >= 0) & (col < n_col * cols)
            )
        return found

    none = [None] * 4
    n0 = cols // (2 * WIN)
    n1 = pcol // WIN
    strip = 4
    flat = strip * cols

    @pl.loop(0, n0)
    def _(j):
        spots = spots0(j)
        scatter(h0, spots, attn_forward(gather(f0, spots), 0, none))

    @pl.loop(0, rows // strip)
    def _(j):
        h = h0[pl.ds(j * strip, strip)].reshape(flat, channels)
        low = feed_forward(h, 0).astype(BF).astype(F32)
        f1[pl.ds(HALF + j * strip, strip), HALF : HALF + cols, :] = low.reshape(
            strip, cols, channels
        )

    def exchange(slot, axis, sends, recvs):
        copies = []
        for way, (step, there) in enumerate(((-1, 1), (1, 0))):
            copy = pltpu.make_async_remote_copy(
                src_ref=sends.at[slot // 2, way],
                dst_ref=recvs.at[slot // 2, there],
                send_sem=halo_send.at[2 * slot + way],
                recv_sem=halo_recv.at[2 * slot + there],
                device_id=side(axis, step),
                device_id_type=MESH,
            )
            copy.start()
            copies.append(copy)
        for copy in copies:
            copy.wait()

    pl.semaphore_wait(barrier, len(greet))

    def put_rows(at, field, first, second):
        hs_row[at, 0] = field[first : first + HALF].reshape(HALF * pcol, channels).astype(BF)
        hs_row[at, 1] = field[second : second + HALF].reshape(HALF * pcol, channels).astype(BF)

    def put_cols(at, field):
        hs_col[at, 0] = field[:, 0:WIN, :].reshape(prow * WIN, channels).astype(BF)
        hs_col[at, 1] = field[:, pcol - WIN : pcol, :].reshape(prow * WIN, channels).astype(BF)

    def got_row(at, way):
        return hr_row[at, way].astype(F32).reshape(HALF, pcol, channels)

    def got_col(at, way):
        return hr_col[at, way].astype(F32).reshape(prow, WIN, channels)

    put_rows(0, f1, HALF, rows)
    exchange(0, "row", hs_row, hr_row)
    f1[0:HALF] = got_row(0, 0)
    f1[prow - HALF : prow] = got_row(0, 1)
    put_cols(0, f1)
    exchange(1, "col", hs_col, hr_col)
    upper_half = lax.broadcasted_iota(jnp.int32, (prow, WIN, channels), 1) >= HALF
    f1[:, 0:WIN, :] = jnp.where(upper_half, f1[:, 0:WIN, :], got_col(0, 0))
    f1[:, pcol - WIN : pcol, :] = jnp.where(
        upper_half, got_col(0, 1), f1[:, pcol - WIN : pcol, :]
    )

    @pl.loop(0, n1)
    def _(j):
        spots = spots1(j)
        scatter(h1, spots, attn_forward(gather(f1, spots), 1, usable1(spots)))

    @pl.loop(0, rows // strip)
    def _(j):
        inner = pl.ds(HALF + j * strip, strip)
        h = h1[inner, HALF : HALF + cols, :].reshape(flat, channels)
        g = cot[pl.ds(j * strip, strip)].astype(F32).reshape(flat, channels)
        result, dh = feed_backward(h, g, 1, True)
        out[pl.ds(j * strip, strip)] = result.reshape(strip, cols, channels).astype(BF)
        dh1[inner, HALF : HALF + cols, :] = dh.reshape(strip, cols, channels)

    @pl.loop(0, n1)
    def _(j):
        spots = spots1(j)
        du = attn_backward(gather(f1, spots), gather(dh1, spots), 1, usable1(spots))
        scatter(g1, spots, du)

    put_cols(1, g1)
    exchange(3, "col", hs_col, hr_col)
    g1[:, 0:WIN, :] += got_col(1, 0)
    g1[:, pcol - WIN : pcol, :] += got_col(1, 1)
    put_rows(1, g1, 0, prow - HALF)
    exchange(2, "row", hs_row, hr_row)
    g1[HALF : 2 * HALF] += got_row(1, 0)
    g1[rows : rows + HALF] += got_row(1, 1)

    @pl.loop(0, rows // strip)
    def _(j):
        here = pl.ds(j * strip, strip)
        h = h0[here].reshape(flat, channels)
        g = g1[pl.ds(HALF + j * strip, strip), HALF : HALF + cols, :].reshape(flat, channels)
        _, dh = feed_backward(h, g, 0, False)
        h0[here] = dh.reshape(strip, cols, channels)

    @pl.loop(0, n0)
    def _(j):
        spots = spots0(j)
        scatter(grad_region, spots, attn_backward(gather(f0, spots), gather(h0, spots), 0, none))

    def stow(unit, x, width):
        n = x.shape[0] // 16
        for t in range((width + 127) // 128):
            part = x[:, t * 128 : min(width, (t + 1) * 128)]
            wide = part.shape[1]
            pack[unit + t * n : unit + (t + 1) * n, :, 0:wide] = part.reshape(n, 16, wide).astype(BF)

    hidden = wup.shape[2]
    for b in range(2):
        base = b * U_BLOCK
        for t in range(3):
            stow(base + U_QKV + 6 * t, a_qkv[b, t], channels)
        stow(base + U_PROJ, a_proj[b], channels)
        stow(base + U_UP, a_up[b], hidden)
        stow(base + U_DOWN, a_down[b], hidden)
        heads = []
        for h in range(3):
            total = None
            for r in range(WIN):
                at = (WIN - 1 - r) * WIN
                part = a_bias[b, r * WIN : (r + 1) * WIN, h * TOK : (h + 1) * TOK]
                pieces = [part, jnp.zeros((WIN, 128 - at - TOK), F32)]
                if at:
                    pieces = [jnp.zeros((WIN, at), F32)] + pieces
                part = jnp.concatenate(pieces, 1)
                total = part if total is None else total + part
            heads.append(total)
        vec = jnp.concatenate([a_vec[b], jnp.zeros((WIN, 128 - channels), F32)], 1)
        sub = lax.broadcasted_iota(jnp.int32, (WIN, 128), 0)
        for t in range(3):
            vec = jnp.where(sub == 5 + t, a_bup[b : b + 1, t * 128 : (t + 1) * 128], vec)
        small = jnp.concatenate([vec] + heads, 0)
        stow(base + U_SMALL, small, 128)

    source = pack
    size_now = units
    at_sem = 0
    for ph, (size, me, partners) in enumerate(groups):
        part = size_now // size
        copies = []
        for d, neg, member, dev in partners:
            copy = pltpu.make_async_remote_copy(
                src_ref=source.at[pl.ds(member * part, part)],
                dst_ref=rs_recv[ph].at[neg - 1],
                send_sem=red_send.at[at_sem + d - 1],
                recv_sem=red_recv.at[at_sem + neg - 1],
                device_id=dev,
                device_id_type=MESH,
            )
            copy.start()
            copies.append(copy)
        total = source[pl.ds(me * part, part)].astype(F32)
        for copy in copies:
            copy.wait()
        for d in range(size - 1):
            total = total + rs_recv[ph][d].astype(F32)
        rs_acc[ph][...] = total.astype(BF)
        source = rs_acc[ph]
        size_now = part
        at_sem += size - 1
    for ph in reversed(range(n_ph)):
        size, me, partners = groups[ph]
        part = size_now
        copies = []
        for d, neg, member, dev in partners:
            copy = pltpu.make_async_remote_copy(
                src_ref=source,
                dst_ref=ag_buf[ph].at[pl.ds(me * part, part)],
                send_sem=red_send.at[at_sem + d - 1],
                recv_sem=red_recv.at[at_sem + neg - 1],
                device_id=dev,
                device_id_type=MESH,
            )
            copy.start()
            copies.append(copy)
        ag_buf[ph][pl.ds(me * part, part)] = source[...]
        for copy in copies:
            copy.wait()
        source = ag_buf[ph]
        size_now = part * size
        at_sem += size - 1

    def fetch(unit, n, width=128):
        return source[unit : unit + n].astype(F32).reshape(n * 16, 128)[:, :width]

    for b in range(2):
        base = b * U_BLOCK
        for t in range(3):
            o_qkv[b, t] = fetch(base + U_QKV + 6 * t, 6, channels)
            o_up[b, :, t * 128 : (t + 1) * 128] = fetch(base + U_UP + 6 * t, 6)
            o_down[b, :, t * 128 : (t + 1) * 128] = fetch(base + U_DOWN + 6 * t, 6)
        o_proj[b] = fetch(base + U_PROJ, 6, channels)
        o_small[b] = fetch(base + U_SMALL, 2)


def expand_table(table):
    side = 2 * WIN - 1
    grid = table.reshape(2, -1, side, side)[:, :, ::-1, ::-1]
    x = jnp.stack([grid[..., WIN - 1 - c : side - c] for c in range(WIN)], 2)
    return x.reshape(2, grid.shape[1], WIN, side * WIN)


def fold_table(dx):
    side = 2 * WIN - 1
    x = dx.reshape(2, -1, WIN, side, WIN)
    total = 0.0
    for c in range(WIN):
        total = total + jnp.pad(
            x[:, :, c], ((0, 0), (0, 0), (0, 0), (WIN - 1 - c, c))
        )
    return total[:, :, ::-1, ::-1].reshape(2, -1, side * side)


def body(n_row, n_col, region, cotangent, gains, wqkv, bqkv, table, wproj, wup, bup, wdown):
    rows, cols, channels = region.shape
    hidden = wup.shape[2]
    prow, pcol = rows + WIN, cols + WIN
    devices = n_row * n_col
    units = -(-2 * U_BLOCK // devices) * devices
    phases = factors(n_row, n_col)
    sizes = []
    for phase in phases:
        size = 1
        for f in phase:
            size *= f[2]
        sizes.append(size)
    recv, acc, gath = [], [], []
    now = units
    for size in sizes:
        gath.append(pltpu.VMEM((now, 16, 128), BF))
        now //= size
        recv.append(pltpu.VMEM((size - 1, now, 16, 128), BF))
        acc.append(pltpu.VMEM((now, 16, 128), BF))
    steps = 2 * sum(s - 1 for s in sizes)
    vmem = pl.BlockSpec(memory_space=pltpu.VMEM)
    shapes = [
        jax.ShapeDtypeStruct((rows, cols, channels), BF),
        jax.ShapeDtypeStruct((rows, cols, channels), F32),
        jax.ShapeDtypeStruct((2, 3, channels, channels), F32),
        jax.ShapeDtypeStruct((2, channels, channels), F32),
        jax.ShapeDtypeStruct((2, channels, hidden), F32),
        jax.ShapeDtypeStruct((2, channels, hidden), F32),
        jax.ShapeDtypeStruct((2, 32, 128), F32),
    ]
    field0 = pltpu.VMEM((rows, cols, channels), F32)
    field1 = pltpu.VMEM((prow, pcol, channels), F32)
    results = pl.pallas_call(
        functools.partial(kernel, n_row, n_col, units),
        out_shape=shapes,
        in_specs=[vmem] * 10,
        out_specs=[vmem] * len(shapes),
        scratch_shapes=[
            pltpu.VMEM((2, 3, channels, channels), BF),
            pltpu.VMEM((2, TOK, 3 * TOK), F32),
            field0,
            field0,
            field1,
            field1,
            field1,
            field1,
            pltpu.VMEM((2, 3, channels, channels), F32),
            pltpu.VMEM((2, channels, channels), F32),
            pltpu.VMEM((2, channels, hidden), F32),
            pltpu.VMEM((2, channels, hidden), F32),
            pltpu.VMEM((2, 8, channels), F32),
            pltpu.VMEM((2, hidden), F32),
            pltpu.VMEM((2, TOK, 3 * TOK), F32),
            pltpu.VMEM((2, 2, HALF * pcol, channels), BF),
            pltpu.VMEM((2, 2, HALF * pcol, channels), BF),
            pltpu.VMEM((2, 2, prow * WIN, channels), BF),
            pltpu.VMEM((2, 2, prow * WIN, channels), BF),
            pltpu.SemaphoreType.DMA((8,)),
            pltpu.SemaphoreType.DMA((8,)),
            pltpu.VMEM((units, 16, 128), BF),
            *recv,
            *acc,
            *gath,
            pltpu.SemaphoreType.DMA((steps,)),
            pltpu.SemaphoreType.DMA((steps,)),
        ],
        compiler_params=pltpu.CompilerParams(
            collective_id=0, has_side_effects=True, vmem_limit_bytes=48 * 1024 * 1024
        ),
        name="swin_pair",
    )(region, cotangent, gains, wqkv, bqkv, expand_table(table), wproj, wup, bup, wdown)
    out, grad_region, dqkv, dproj, dup, down_t, small = results
    vec = small[:, 0:5, :channels]
    return (
        out,
        grad_region,
        vec[:, 3:5],
        dqkv.transpose(0, 2, 1, 3).reshape(2, channels, 3 * channels),
        vec[:, 0:3].reshape(2, 3 * channels),
        fold_table(small[:, 8:32, : (2 * WIN - 1) * WIN].reshape(2, 3, WIN, -1)),
        dproj,
        dup,
        small[:, 5:8].reshape(2, hidden),
        down_t.transpose(0, 2, 1),
    )


def solution(mesh):
    tile = P("row", "col", None)
    return jax.shard_map(
        functools.partial(body, mesh.shape["row"], mesh.shape["col"]),
        mesh=mesh,
        in_specs=(tile, tile) + (P(),) * 8,
        out_specs=(tile, tile) + (P(),) * 8,
        check_vma=False,
    )
```

time: 319 us -> 105 us (0.33)
  waiting for transfers between devices: 135 us -> 0 us
  Pallas kernels: 0 us -> 92.1 us
  local copies, waits for them, and re-layouts: 84.4 us -> 11.8 us
  matrix products: 37 us -> 0 us
  other arithmetic: 25.1 us -> 0.16 us
  starting transfers between devices: 19.7 us -> 0 us
  between operations: 16 us -> 0.89 us
    psum x1 -> x0, waiting for transfers between devices: 133 us -> none  [body(): lax.psum((lower_flat, upper_flat), ('row', 'col'))]
    pallas_call x0 -> x1, Pallas kernels: none -> 92.1 us  [body(): pl.pallas_call(functools.partial(kernel, n_row, n_col, units), out_shape=...]
    dot_general x38 -> x0, matrix products: 34 us -> none  [the longest x4 8.48 us: position_bias(): return jnp.einsum('qkt,ht->hqk', onehot, table, precision=HIGHEST)]
    reshape x30 -> x4, local copies, waits for them, and re-layouts: 26.9 us -> 2.13 us  [the longest x1 0.78 us: expand_table(): grid = table.reshape(2, -1, side, side)[:, :, ::-1, ::-1]]
    ppermute x8 -> x0, starting transfers between devices: 19.6 us -> none  [the longest x4 14.5 us: padded_2(): before = lax.ppermute(last, axis, up)]
    concatenate x2 -> x0, local copies, waits for them, and re-layouts: 15.5 us -> none  [flatten(): jnp.concatenate([part.astype(jnp.float32).reshape(-1) for part in parts])]
    slice x24 -> x12, local copies, waits for them, and re-layouts: 15.5 us -> 1.61 us  [the longest x9 1.02 us: expand_table(): x = jnp.stack([grid[..., WIN - 1 - c:side - c] for c in range(WIN)], 2)]
    reduce_sum x18 -> x0, other arithmetic: 11.4 us -> none  [the longest x4 3.41 us: layer_norm(): variance = jnp.mean(centred * centred, -1, keepdims=True)]
  transfers between devices with their start and end apart: 9 -> 0, of which waited for: 2 -> 0; matrix products, arithmetic and copies ran while one was open for 7% -> 0% of each run, Pallas kernels for 0% -> 0%
where the time goes in v1:
time: 105 us
  Pallas kernels  92.1 us (88%)
  local copies, waits for them, and re-layouts  11.8 us (11%)
    pallas_call x1, Pallas kernels, body(): pl.pallas_call(functools.partial(kernel, n_row, n_col, units), out_shape=...  92.1 us
    unnamed x25, local copies, waits for them, and re-layouts  6.72 us

profile of v1, /device:TPU:0, one launch (start us, length us, event | category | flops | bytes accessed | tf_op | source)
XLA Modules:
  0.0 104.9 jit_solution(10470719289855889092)
XLA Ops:
  0.6 0.8 reshape.52
  1.4 1.1 %copy.45.wdown = bf16[2,384,96]{2,1,0:T(8,128)(2,1)S(1)} copy(bf16[2,384,96]{1,2,0:T(8,128)(2,1)} %param.19) | data formatting | bytes 294912 | tf_op args[9]
  2.5 0.2 fusion
  2.7 0.1 slice.102
  2.9 0.1 slice.100
  4.3 0.1 slice.88
  4.6 0.3 copy-done.1
  4.9 0.1 copy-done
  5.0 0.2 copy-done.5
  5.3 92.1 %swin_pair.1 = (bf16[16,48,96]{2,1,0:T(8,128)(2,1)S(1)}, f32[16,48,96]{2,1,0:T(8,128)S(1)}, f32[2,3,96,96]{3,2,1,0:T(8,128)S(1)}, f32[2,96,96]{2,1,0:T(8,128)S(1...) custom-call(bf16[16,48,96]{2,1,0:T(8,128)(2,1)S(1)} %copy-done, ...), custom_call_target="tpu_custom_call" | custom-call | tf_op jit(solution)/shard_map/swin_pair/pallas_call | solution.py:590
  97.3 0.6 slice.103
  97.9 0.6 copy.66
  98.5 0.7 reshape.54
  99.2 0.1 copy.46
  99.3 0.9 copy.55
  100.2 0.2 reshape_reshape.3
  100.5 0.2 pad_add_fusion
  100.6 0.1 rev.4
  100.8 0.6 copy.56
  101.4 0.7 copy.72
  102.1 0.7 copy.73
  102.9 0.6 copy.74
  103.5 0.7 copy.75
  104.2 0.7 copy.76
  (40 shorter events, 1.6 us)
Async XLA Ops:
  3.3 1.2 %copy-start.4 = (bf16[2,96,96]{2,1,0:T(8,128)(2,1)S(1)}, bf16[2,96,96]{2,1,0:T(8,128)(2,1)}, u32[]{:S(2)}) copy-start(bf16[2,96,96]{2,1,0:T(8,128)(2,1)} %wproj.1) | copy-start | bytes 110596
  3.5 1.1 %copy-start.3 = (bf16[2,96,384]{2,1,0:T(8,128)(2,1)S(1)}, bf16[2,96,384]{2,1,0:T(8,128)(2,1)}, u32[]{:S(2)}) copy-start(bf16[2,96,384]{2,1,0:T(8,128)(2,1)} %wup.1) | copy-start | bytes 442372
  3.7 0.9 copy-start.2
  3.9 1.0 copy-start.1
  4.0 1.0 copy-start
  4.5 0.7 copy-start.5
  4.5 0.7 copy-start.6
  4.5 0.7 copy-start.7

commit v2 on v1

--- a/solution.py
+++ b/solution.py
@@ -13,6 +13,7 @@
 BF = jnp.bfloat16
 F32 = jnp.float32
 MESH = pl.DeviceIdType.MESH
+GROUP = 6
 
 U_QKV = 0
 U_PROJ = 18
@@ -48,30 +49,19 @@
     )
 
 
-def seg_first(shape):
-    return lax.broadcasted_iota(jnp.int32, shape, 1) < TOK
-
-
-def seg_reduce(fn, fill, s):
-    lo, hi = s[:, :128], s[:, 128:]
-    first = seg_first(lo.shape)
-    r0 = fn(jnp.where(first, lo, fill), -1, keepdims=True)
-    r1 = fn(jnp.where(first, fill, lo), -1, keepdims=True)
-    r2 = fn(hi, -1, keepdims=True)
-    return r0, r1, r2
-
-
-def seg_spread(parts, like):
-    r0, r1, r2 = parts
-    lo = jnp.where(seg_first((like.shape[0], 128)), r0, r1)
-    hi = jnp.broadcast_to(r2, (like.shape[0], 64))
-    return jnp.concatenate([lo, hi], 1)
+def per_head(fn, x):
+    return [fn(x[h * TOK : (h + 1) * TOK], 0, keepdims=True) for h in range(3)]
+
+
+def by_head(op, x, parts):
+    return jnp.concatenate(
+        [op(x[h * TOK : (h + 1) * TOK], parts[h]) for h in range(3)], 0
+    )
 
 
 def softmax(s):
-    e = jnp.exp(s - seg_spread(seg_reduce(jnp.max, -jnp.inf, s), s))
-    sums = seg_reduce(jnp.sum, 0.0, e)
-    return e * seg_spread(tuple(1.0 / t for t in sums), s)
+    e = by_head(lambda x, top: jnp.exp(x - top), s, per_head(jnp.max, s))
+    return by_head(lambda x, total: x * (1.0 / total), e, per_head(jnp.sum, e))
 
 
 def head_masks(channels):
@@ -141,10 +131,24 @@
     halo_send,
     halo_recv,
     pack,
+    sq,
+    sk,
+    sv,
+    sp,
+    smix,
+    sa,
+    sx,
+    sr,
+    fx,
+    fr,
+    ff,
+    fm,
+    fs,
     *rest,
 ):
     rows, cols, channels = region.shape
     prow, pcol = rows + WIN, cols + WIN
+    wide = pcol + WIN
     scale = (channels // 3) ** (-0.5)
     phases = factors(n_row, n_col)
     n_ph = len(phases)
@@ -209,9 +213,11 @@
             ws[b, t] = whole[:, t * channels : (t + 1) * channels].astype(BF)
         for r in range(WIN):
             at = (WIN - 1 - r) * WIN
-            bias[b, r * WIN : (r + 1) * WIN, :] = jnp.concatenate(
-                [xtab[b, h][:, at : at + TOK] for h in range(3)], 1
-            )
+            for h in range(3):
+                part = xtab[b, h][:, at : at + TOK]
+                bias[b, h * TOK + r * WIN : h * TOK + (r + 1) * WIN, :] = jnp.concatenate(
+                    [part, part], 1
+                )
     f0[...] = region[...].astype(F32)
     masks = head_masks(channels)
 
@@ -225,45 +231,61 @@
         ]
         return xhat, rstd, a, parts
 
-    def window(q, k, v, b, usable):
-        kbd, vbd = stack_heads(k, masks), stack_heads(v, masks)
-        s = dot_nt(q, kbd) * scale + bias[b]
-        if usable is not None:
-            s = jnp.where(usable, s, -1e30)
-        return kbd, vbd, softmax(s)
-
     def split(x, w):
         return x[w * TOK : (w + 1) * TOK]
 
-    def attn_forward(u, b, usable):
-        _, _, _, (q, k, v) = qkv_of(u, b)
+    left = lax.broadcasted_iota(jnp.int32, (3 * TOK, 2 * TOK), 1) < TOK
+
+    def pair_product(first, second, both):
+        return jnp.where(left, dot_nt(first, both), dot_nt(second, both))
+
+    def pair_rows(x, first, second):
+        return jnp.concatenate([dot_tn(x, first)[:TOK], dot_tn(x, second)[TOK:]], 0)
+
+    def pair_sum(x, both):
+        rest_rows = jnp.zeros_like(both[:TOK])
+        one = dot_nn(x, jnp.concatenate([both[:TOK], rest_rows], 0))
+        two = dot_nn(x, jnp.concatenate([rest_rows, both[TOK:]], 0))
+        return [fold_heads(one, masks), fold_heads(two, masks)]
+
+    def stacked(x, w):
+        return stack_heads(split(x, w), masks), stack_heads(split(x, w + 1), masks)
+
+    def attn_forward(u, b, at, usable):
+        xhat, rstd, a, (q, k, v) = qkv_of(u, b)
+        sq[at], sk[at], sv[at], sa[at] = q, k, v, a
+        sx[at] = xhat
+        sr[at] = jnp.broadcast_to(rstd, xhat.shape)
         mixed = []
-        for w in range(u.shape[0] // TOK):
-            _, vbd, p = window(split(q, w), split(k, w), split(v, w), b, usable[w])
-            mixed.append(dot_nn(p.astype(BF), vbd))
+        for w in range(0, GROUP, 2):
+            both = q[w * TOK : (w + 2) * TOK]
+            s = pair_product(*stacked(k, w), both) * scale + bias[b]
+            if usable is not None:
+                s = jnp.where(usable(w), s, -1e30)
+            p = softmax(s)
+            sp[at, w // 2] = p
+            mixed.append(pair_rows(p.astype(BF), *stacked(v, w)))
         mixed = jnp.concatenate(mixed, 0).astype(BF)
+        smix[at] = mixed
         return u + dot_nn(mixed, wproj[b])
 
-    def attn_backward(u, dh, b, usable):
-        xhat, rstd, a, (q, k, v) = qkv_of(u, b)
+    def attn_backward(dh, b, at):
+        xhat, rstd, a, q, k, v = sx[at], sr[at], sa[at], sq[at], sk[at], sv[at]
         dhb = dh.astype(BF)
         dmix = dot_nt(dhb, wproj[b]).astype(BF)
-        mixed, dqs, dks, dvs = [], [], [], []
+        a_proj[b] += dot_tn(smix[at], dhb)
+        dqs, dks, dvs = [], [], []
         dbias = None
-        for w in range(u.shape[0] // TOK):
-            qw, do = split(q, w), split(dmix, w)
-            kbd, vbd, p = window(qw, split(k, w), split(v, w), b, usable[w])
-            pb = p.astype(BF)
-            mixed.append(dot_nn(pb, vbd))
-            dp = dot_nt(do, vbd)
-            ds = p * (dp - seg_spread(seg_reduce(jnp.sum, 0.0, dp * p), p))
+        for w in range(0, GROUP, 2):
+            both, do = q[w * TOK : (w + 2) * TOK], dmix[w * TOK : (w + 2) * TOK]
+            p = sp[at, w // 2]
+            dp = pair_product(*stacked(v, w), do)
+            ds = p * by_head(jnp.subtract, dp, per_head(jnp.sum, dp * p))
             dbias = ds if dbias is None else dbias + ds
             dsb = (ds * scale).astype(BF)
-            dqs.append(dot_nn(dsb, kbd))
-            dks.append(fold_heads(dot_tn(dsb, qw), masks))
-            dvs.append(fold_heads(dot_tn(pb, do), masks))
-        mixed = jnp.concatenate(mixed, 0).astype(BF)
-        a_proj[b] += dot_tn(mixed, dhb)
+            dqs.append(pair_rows(dsb, *stacked(k, w)))
+            dks += pair_sum(dsb, both)
+            dvs += pair_sum(p.astype(BF), do)
         a_bias[b] += dbias
         da = None
         for t, parts in enumerate((dqs, dks, dvs)):
@@ -280,38 +302,44 @@
         t = jnp.tanh(0.7978845608028654 * z * (1.0 + 0.044715 * z * z))
         return t, 0.5 * z * (1.0 + t)
 
+    def slope_of(z, t):
+        return 0.5 * (1.0 + t) + 0.5 * z * (1.0 - t * t) * (
+            0.7978845608028654 * (1.0 + 0.134145 * z * z)
+        )
+
     def feed_forward(h, b):
-        xhat, _ = norm(h)
-        f = (xhat * gains[b, 1:2, :]).astype(BF)
-        _, m = gelu(dot_nn(f, wup[b]) + bup[b : b + 1, :])
-        return h + dot_nn(m.astype(BF), wdown[b])
-
-    def feed_backward(h, g, b, want_out):
         xhat, rstd = norm(h)
         f = (xhat * gains[b, 1:2, :]).astype(BF)
         z = dot_nn(f, wup[b]) + bup[b : b + 1, :]
         t, m = gelu(z)
         m = m.astype(BF)
-        result = h + dot_nn(m, wdown[b]) if want_out else None
+        return h + dot_nt(m, wdown[b]), (xhat, rstd, f, m, slope_of(z, t))
+
+    def feed_backward(saved, g, b):
+        xhat, rstd, f, m, slope = saved
         gb = g.astype(BF)
-        dm = dot_nt(gb, wdown[b])
-        slope = 0.5 * (1.0 + t) + 0.5 * z * (1.0 - t * t) * (
-            0.7978845608028654 * (1.0 + 0.134145 * z * z)
-        )
-        dz = dm * slope
+        dz = dot_nn(gb, wdown[b]) * slope
         a_bup[b : b + 1, :] += jnp.sum(dz, 0, keepdims=True)
         dz = dz.astype(BF)
         a_down[b] += dot_tn(gb, m)
         a_up[b] += dot_tn(f, dz)
         df = dot_nt(dz, wup[b])
         a_vec[b, 4:5, :] += jnp.sum(df * xhat, 0, keepdims=True)
-        return result, g + norm_back(df, gains[b, 1:2, :], xhat, rstd)
+        return g + norm_back(df, gains[b, 1:2, :], xhat, rstd)
 
     def spots0(j):
-        return [(i * WIN, pl.multiple_of((j * 2 + c) * WIN, WIN)) for i in range(rows // WIN) for c in range(2)]
+        return [
+            (i * WIN, pl.multiple_of((j * 3 + c) * WIN, WIN))
+            for i in range(rows // WIN)
+            for c in range(3)
+        ]
 
     def spots1(j):
-        return [(i * WIN, pl.multiple_of(j * WIN, WIN)) for i in range(prow // WIN)]
+        return [
+            (i * WIN, pl.multiple_of((j * 2 + c) * WIN, WIN))
+            for i in range(prow // WIN)
+            for c in range(2)
+        ]
 
     def gather(ref, spots):
         return jnp.concatenate(
@@ -322,35 +350,35 @@
         for w, (r, c) in enumerate(spots):
             ref[r : r + WIN, pl.ds(c, WIN), :] = split(x, w).reshape(WIN, WIN, channels)
 
-    lane = lax.broadcasted_iota(jnp.int32, (1, 3 * TOK), 1)
-    key_row = lax.div(lax.rem(lane, TOK), WIN)
-    key_col = lax.rem(lane, WIN)
-
-    def usable1(spots):
-        found = []
-        for r, c in spots:
-            row = key_row + (index["row"] * rows - HALF + r)
-            col = key_col + (index["col"] * cols - HALF + c)
-            found.append(
-                (row >= 0) & (row < n_row * rows) & (col >= 0) & (col < n_col * cols)
-            )
-        return found
-
-    none = [None] * 4
-    n0 = cols // (2 * WIN)
-    n1 = pcol // WIN
+    key = lax.broadcasted_iota(jnp.int32, (3 * TOK, 2 * TOK), 0)
+    key_row = lax.div(lax.rem(key, TOK), WIN) + (index["row"] * rows - HALF)
+    key_col = lax.rem(key, WIN) + jnp.where(left, 0, WIN) + (index["col"] * cols - HALF)
+
+    def usable1(j):
+        def usable(w):
+            row = key_row + (w // 2) * WIN
+            col = key_col + j * (2 * WIN)
+            return (row >= 0) & (row < n_row * rows) & (col >= 0) & (col < n_col * cols)
+
+        return usable
+
+    n0 = cols // (3 * WIN)
+    n1 = wide // (2 * WIN)
     strip = 4
     flat = strip * cols
 
     @pl.loop(0, n0)
     def _(j):
         spots = spots0(j)
-        scatter(h0, spots, attn_forward(gather(f0, spots), 0, none))
+        scatter(h0, spots, attn_forward(gather(f0, spots), 0, j, None))
 
     @pl.loop(0, rows // strip)
     def _(j):
         h = h0[pl.ds(j * strip, strip)].reshape(flat, channels)
-        low = feed_forward(h, 0).astype(BF).astype(F32)
+        low, (xhat, rstd, f, m, slope) = feed_forward(h, 0)
+        fx[j], ff[j], fm[j], fs[j] = xhat, f, m, slope
+        fr[j] = jnp.broadcast_to(rstd, xhat.shape)
+        low = low.astype(BF).astype(F32)
         f1[pl.ds(HALF + j * strip, strip), HALF : HALF + cols, :] = low.reshape(
             strip, cols, channels
         )
@@ -374,8 +402,8 @@
     pl.semaphore_wait(barrier, len(greet))
 
     def put_rows(at, field, first, second):
-        hs_row[at, 0] = field[first : first + HALF].reshape(HALF * pcol, channels).astype(BF)
-        hs_row[at, 1] = field[second : second + HALF].reshape(HALF * pcol, channels).astype(BF)
+        hs_row[at, 0] = field[first : first + HALF, 0:pcol, :].reshape(HALF * pcol, channels).astype(BF)
+        hs_row[at, 1] = field[second : second + HALF, 0:pcol, :].reshape(HALF * pcol, channels).astype(BF)
 
     def put_cols(at, field):
         hs_col[at, 0] = field[:, 0:WIN, :].reshape(prow * WIN, channels).astype(BF)
@@ -389,8 +417,8 @@
 
     put_rows(0, f1, HALF, rows)
     exchange(0, "row", hs_row, hr_row)
-    f1[0:HALF] = got_row(0, 0)
-    f1[prow - HALF : prow] = got_row(0, 1)
+    f1[0:HALF, 0:pcol, :] = got_row(0, 0)
+    f1[prow - HALF : prow, 0:pcol, :] = got_row(0, 1)
     put_cols(0, f1)
     exchange(1, "col", hs_col, hr_col)
     upper_half = lax.broadcasted_iota(jnp.int32, (prow, WIN, channels), 1) >= HALF
@@ -402,22 +430,22 @@
     @pl.loop(0, n1)
     def _(j):
         spots = spots1(j)
-        scatter(h1, spots, attn_forward(gather(f1, spots), 1, usable1(spots)))
+        scatter(h1, spots, attn_forward(gather(f1, spots), 1, n0 + j, usable1(j)))
 
     @pl.loop(0, rows // strip)
     def _(j):
         inner = pl.ds(HALF + j * strip, strip)
         h = h1[inner, HALF : HALF + cols, :].reshape(flat, channels)
         g = cot[pl.ds(j * strip, strip)].astype(F32).reshape(flat, channels)
-        result, dh = feed_backward(h, g, 1, True)
+        result, saved = feed_forward(h, 1)
+        dh = feed_backward(saved, g, 1)
         out[pl.ds(j * strip, strip)] = result.reshape(strip, cols, channels).astype(BF)
         dh1[inner, HALF : HALF + cols, :] = dh.reshape(strip, cols, channels)
 
     @pl.loop(0, n1)
     def _(j):
         spots = spots1(j)
-        du = attn_backward(gather(f1, spots), gather(dh1, spots), 1, usable1(spots))
-        scatter(g1, spots, du)
+        scatter(g1, spots, attn_backward(gather(dh1, spots), 1, n0 + j))
 
     put_cols(1, g1)
     exchange(3, "col", hs_col, hr_col)
@@ -425,21 +453,20 @@
     g1[:, pcol - WIN : pcol, :] += got_col(1, 1)
     put_rows(1, g1, 0, prow - HALF)
     exchange(2, "row", hs_row, hr_row)
-    g1[HALF : 2 * HALF] += got_row(1, 0)
-    g1[rows : rows + HALF] += got_row(1, 1)
+    g1[HALF : 2 * HALF, 0:pcol, :] += got_row(1, 0)
+    g1[rows : rows + HALF, 0:pcol, :] += got_row(1, 1)
 
     @pl.loop(0, rows // strip)
     def _(j):
         here = pl.ds(j * strip, strip)
-        h = h0[here].reshape(flat, channels)
         g = g1[pl.ds(HALF + j * strip, strip), HALF : HALF + cols, :].reshape(flat, channels)
-        _, dh = feed_backward(h, g, 0, False)
+        dh = feed_backward((fx[j], fr[j], ff[j], fm[j], fs[j]), g, 0)
         h0[here] = dh.reshape(strip, cols, channels)
 
     @pl.loop(0, n0)
     def _(j):
         spots = spots0(j)
-        scatter(grad_region, spots, attn_backward(gather(f0, spots), gather(h0, spots), 0, none))
+        scatter(grad_region, spots, attn_backward(gather(h0, spots), 0, j))
 
     def stow(unit, x, width):
         n = x.shape[0] // 16
@@ -461,7 +488,9 @@
             total = None
             for r in range(WIN):
                 at = (WIN - 1 - r) * WIN
-                part = a_bias[b, r * WIN : (r + 1) * WIN, h * TOK : (h + 1) * TOK]
+                line = h * TOK + r * WIN
+                part = a_bias[b, line : line + WIN, :]
+                part = part[:, :TOK] + part[:, TOK:]
                 pieces = [part, jnp.zeros((WIN, 128 - at - TOK), F32)]
                 if at:
                     pieces = [jnp.zeros((WIN, at), F32)] + pieces
@@ -538,7 +567,7 @@
 
 def expand_table(table):
     side = 2 * WIN - 1
-    grid = table.reshape(2, -1, side, side)[:, :, ::-1, ::-1]
+    grid = table.reshape(2, -1, side, side)
     x = jnp.stack([grid[..., WIN - 1 - c : side - c] for c in range(WIN)], 2)
     return x.reshape(2, grid.shape[1], WIN, side * WIN)
 
@@ -551,7 +580,7 @@
         total = total + jnp.pad(
             x[:, :, c], ((0, 0), (0, 0), (0, 0), (WIN - 1 - c, c))
         )
-    return total[:, :, ::-1, ::-1].reshape(2, -1, side * side)
+    return total.reshape(2, -1, side * side)
 
 
 def body(n_row, n_col, region, cotangent, gains, wqkv, bqkv, table, wproj, wup, bup, wdown):
@@ -574,6 +603,7 @@
         now //= size
         recv.append(pltpu.VMEM((size - 1, now, 16, 128), BF))
         acc.append(pltpu.VMEM((now, 16, 128), BF))
+    turns = cols // (3 * WIN) + (pcol + WIN) // (2 * WIN)
     steps = 2 * sum(s - 1 for s in sizes)
     vmem = pl.BlockSpec(memory_space=pltpu.VMEM)
     shapes = [
@@ -586,7 +616,7 @@
         jax.ShapeDtypeStruct((2, 32, 128), F32),
     ]
     field0 = pltpu.VMEM((rows, cols, channels), F32)
-    field1 = pltpu.VMEM((prow, pcol, channels), F32)
+    field1 = pltpu.VMEM((prow, pcol + WIN, channels), F32)
     results = pl.pallas_call(
         functools.partial(kernel, n_row, n_col, units),
         out_shape=shapes,
@@ -594,7 +624,7 @@
         out_specs=[vmem] * len(shapes),
         scratch_shapes=[
             pltpu.VMEM((2, 3, channels, channels), BF),
-            pltpu.VMEM((2, TOK, 3 * TOK), F32),
+            pltpu.VMEM((2, 3 * TOK, 2 * TOK), F32),
             field0,
             field0,
             field1,
@@ -607,7 +637,7 @@
             pltpu.VMEM((2, channels, hidden), F32),
             pltpu.VMEM((2, 8, channels), F32),
             pltpu.VMEM((2, hidden), F32),
-            pltpu.VMEM((2, TOK, 3 * TOK), F32),
+            pltpu.VMEM((2, 3 * TOK, 2 * TOK), F32),
             pltpu.VMEM((2, 2, HALF * pcol, channels), BF),
             pltpu.VMEM((2, 2, HALF * pcol, channels), BF),
             pltpu.VMEM((2, 2, prow * WIN, channels), BF),
@@ -615,6 +645,14 @@
             pltpu.SemaphoreType.DMA((8,)),
             pltpu.SemaphoreType.DMA((8,)),
             pltpu.VMEM((units, 16, 128), BF),
+            *[pltpu.VMEM((turns, GROUP * TOK, channels), BF)] * 3,
+            pltpu.VMEM((turns, GROUP // 2, 3 * TOK, 2 * TOK), F32),
+            *[pltpu.VMEM((turns, GROUP * TOK, channels), BF)] * 2,
+            *[pltpu.VMEM((turns, GROUP * TOK, channels), F32)] * 2,
+            *[pltpu.VMEM((rows // 4, 4 * cols, channels), F32)] * 2,
+            pltpu.VMEM((rows // 4, 4 * cols, channels), BF),
+            pltpu.VMEM((rows // 4, 4 * cols, hidden), BF),
+            pltpu.VMEM((rows // 4, 4 * cols, hidden), F32),
             *recv,
             *acc,
             *gath,
@@ -625,7 +663,7 @@
             collective_id=0, has_side_effects=True, vmem_limit_bytes=48 * 1024 * 1024
         ),
         name="swin_pair",
-    )(region, cotangent, gains, wqkv, bqkv, expand_table(table), wproj, wup, bup, wdown)
+    )(region, cotangent, gains, wqkv, bqkv, expand_table(table), wproj, wup, bup, wdown.transpose(0, 2, 1))
     out, grad_region, dqkv, dproj, dup, down_t, small = results
     vec = small[:, 0:5, :channels]
     return (

time: 105 us -> 76 us (0.72)
  Pallas kernels: 92.1 us -> 65.1 us
  local copies, waits for them, and re-layouts: 11.8 us -> 9.7 us
    pallas_call x1, Pallas kernels: 92.1 us -> 65.1 us  [body(): pl.pallas_call(functools.partial(kernel, n_row, n_col, units), out_shape=...]
    unnamed x25 -> x26, local copies, waits for them, and re-layouts: 6.72 us -> 5.61 us
where the time goes in v2:
time: 76 us; the launch traced here: 75.8 us
  Pallas kernels  65.1 us (86%)
  local copies, waits for them, and re-layouts  9.7 us (13%)
  between operations  0.87 us (1%)
    pallas_call x1, Pallas kernels, body(): pl.pallas_call(functools.partial(kernel, n_row, n_col, units), out_shape=...  65.1 us
    unnamed x26, local copies, waits for them, and re-layouts  5.61 us

profile of v2, /device:TPU:0, one launch (start us, length us, event | category | flops | bytes accessed | tf_op | source)
XLA Modules:
  0.0 75.8 jit_solution(4119270551972095896)
XLA Ops:
  0.6 0.8 %reshape.52 = f32[2,3,15,15]{3,2,0,1:T(8,128)S(1)} reshape(f32[2,3,225]{2,0,1:T(2,128)} %param.15) | data formatting | bytes 10800 | tf_op jit(solution)/shard_map/reshape | solution.py:570
  1.5 0.1 fusion
  1.6 0.1 stack.34
  1.8 0.1 stack.33
  2.2 0.1 stack.29
  2.3 0.1 stack.28
  2.4 0.1 stack.27
  2.6 0.2 copy-done
  2.8 0.1 copy-done.1
  2.9 0.3 copy-done.6
  3.3 65.1 %swin_pair.1 = (bf16[16,48,96]{2,1,0:T(8,128)(2,1)S(1)}, f32[16,48,96]{2,1,0:T(8,128)S(1)}, f32[2,3,96,96]{3,2,1,0:T(8,128)S(1)}, f32[2,96,96]{2,1,0:T(8,128)S(1...) custom-call(bf16[16,48,96]{2,1,0:T(8,128)(2,1)S(1)} %copy-done, ...), custom_call_target="tpu_custom_call" | custom-call | tf_op jit(solution)/shard_map/swin_pair/pallas_call | solution.py:620
  68.3 0.6 slice.71
  68.9 0.6 copy.64
  69.5 0.7 reshape.54
  70.2 0.1 copy.44
  70.3 0.9 %copy.53 = f32[2,96,288]{2,1,0:T(8,128)} copy(f32[2,96,288]{1,2,0:T(8,128)S(1)} %bitcast.60) | data formatting | bytes 442368
  71.2 0.2 reshape_reshape.3
  71.4 0.2 pad_add_fusion
  71.7 0.6 copy.54
  72.3 0.7 copy.70
  73.0 0.7 copy.71
  73.7 0.6 copy.72
  74.4 0.7 copy.73
  75.1 0.7 copy.74
  (32 shorter events, 0.6 us)
Async XLA Ops:
  1.4 1.2 %copy-start.2 = (bf16[2,96,288]{2,1,0:T(8,128)(2,1)S(1)}, bf16[2,96,288]{2,1,0:T(8,128)(2,1)}, u32[]{:S(2)}) copy-start(bf16[2,96,288]{2,1,0:T(8,128)(2,1)} %wqkv.1) | copy-start | bytes 331780
  1.4 1.2 %copy-start.3 = (bf16[2,96,384]{2,1,0:T(8,128)(2,1)S(1)}, bf16[2,96,384]{2,1,0:T(8,128)(2,1)}, u32[]{:S(2)}) copy-start(bf16[2,96,384]{2,1,0:T(8,128)(2,1)} %wup.1) | copy-start | bytes 442372
  1.5 1.2 %copy-start.4 = (bf16[2,384,96]{1,2,0:T(8,128)(2,1)S(1)}, bf16[2,384,96]{1,2,0:T(8,128)(2,1)}, u32[]{:S(2)}) copy-start(bf16[2,384,96]{1,2,0:T(8,128)(2,1)} %param.19) | copy-start | bytes 442372
  1.7 0.9 %copy-start.5 = (bf16[2,96,96]{2,1,0:T(8,128)(2,1)S(1)}, bf16[2,96,96]{2,1,0:T(8,128)(2,1)}, u32[]{:S(2)}) copy-start(bf16[2,96,96]{2,1,0:T(8,128)(2,1)} %wproj.1) | copy-start | bytes 110596
  1.7 0.9 %copy-start.7 = (f32[2,384]{1,0:T(2,128)S(1)}, f32[2,384]{1,0:T(2,128)}, u32[]{:S(2)}) copy-start(f32[2,384]{1,0:T(2,128)} %bup.1) | copy-start | bytes 9220
  1.9 1.0 %copy-start = (bf16[16,48,96]{2,1,0:T(8,128)(2,1)S(1)}, bf16[16,48,96]{2,1,0:T(8,128)(2,1)}, u32[]{:S(2)}) copy-start(bf16[16,48,96]{2,1,0:T(8,128)(2,1)} %region.1) | copy-start | bytes 442372
  1.9 1.1 %copy-start.1 = (bf16[16,48,96]{2,1,0:T(8,128)(2,1)S(1)}, bf16[16,48,96]{2,1,0:T(8,128)(2,1)}, u32[]{:S(2)}) copy-start(bf16[16,48,96]{2,1,0:T(8,128)(2,1)} %cot.1) | copy-start | bytes 442372
  2.5 0.7 copy-start.6
  2.5 0.7 copy-start.8

commit v3 on v2

--- a/solution.py
+++ b/solution.py
@@ -80,6 +80,15 @@
     for h in (1, 2):
         out = out + jnp.where(masks[h], x[h * TOK : (h + 1) * TOK], 0.0)
     return out
+
+
+def offsets(c):
+    side = 2 * WIN - 1
+    shape = (side * side, 128)
+    lane = lax.broadcasted_iota(jnp.int32, shape, 1)
+    entry = lax.broadcasted_iota(jnp.int32, shape, 0)
+    wanted = lax.div(lane, WIN) * side + lax.rem(lane, WIN) + (WIN - 1 - c)
+    return jnp.where((entry == wanted) & (lane < side * WIN), 1.0, 0.0).astype(BF)
 
 
 def factors(n_row, n_col):
@@ -97,19 +106,17 @@
     gains,
     wqkv,
     bqkv,
-    xtab,
+    table,
     wproj,
     wup,
     bup,
     wdown,
     out,
     grad_region,
-    o_qkv,
-    o_proj,
-    o_up,
-    o_down,
-    o_small,
+    o_low,
+    o_high,
     ws,
+    xtab,
     bias,
     f0,
     h0,
@@ -207,6 +214,16 @@
 
     for ref in (a_qkv, a_proj, a_up, a_down, a_vec, a_bup, a_bias, dh1, f1, pack):
         ref[...] = jnp.zeros(ref.shape, ref.dtype)
+    terms = []
+    left_over = table[...].reshape(6, table.shape[2])
+    for _ in range(3):
+        terms.append(left_over.astype(BF))
+        left_over = left_over - terms[-1].astype(F32)
+    for c in range(WIN):
+        hot = offsets(c)
+        line = dot_nn(terms[0], hot) + dot_nn(terms[1], hot) + dot_nn(terms[2], hot)
+        for n in range(6):
+            xtab[n // 3, n % 3, c : c + 1, :] = line[n : n + 1]
     for b in range(2):
         whole = wqkv[b].astype(F32)
         for t in range(3):
@@ -329,14 +346,14 @@
 
     def spots0(j):
         return [
-            (i * WIN, pl.multiple_of((j * 3 + c) * WIN, WIN))
+            (i * WIN, (j * 3 + c) * WIN)
             for i in range(rows // WIN)
             for c in range(3)
         ]
 
     def spots1(j):
         return [
-            (i * WIN, pl.multiple_of((j * 2 + c) * WIN, WIN))
+            (i * WIN, (j * 2 + c) * WIN)
             for i in range(prow // WIN)
             for c in range(2)
         ]
@@ -367,122 +384,20 @@
     strip = 4
     flat = strip * cols
 
-    @pl.loop(0, n0)
-    def _(j):
-        spots = spots0(j)
-        scatter(h0, spots, attn_forward(gather(f0, spots), 0, j, None))
-
-    @pl.loop(0, rows // strip)
-    def _(j):
-        h = h0[pl.ds(j * strip, strip)].reshape(flat, channels)
-        low, (xhat, rstd, f, m, slope) = feed_forward(h, 0)
-        fx[j], ff[j], fm[j], fs[j] = xhat, f, m, slope
-        fr[j] = jnp.broadcast_to(rstd, xhat.shape)
-        low = low.astype(BF).astype(F32)
-        f1[pl.ds(HALF + j * strip, strip), HALF : HALF + cols, :] = low.reshape(
-            strip, cols, channels
-        )
-
-    def exchange(slot, axis, sends, recvs):
-        copies = []
-        for way, (step, there) in enumerate(((-1, 1), (1, 0))):
-            copy = pltpu.make_async_remote_copy(
-                src_ref=sends.at[slot // 2, way],
-                dst_ref=recvs.at[slot // 2, there],
-                send_sem=halo_send.at[2 * slot + way],
-                recv_sem=halo_recv.at[2 * slot + there],
-                device_id=side(axis, step),
-                device_id_type=MESH,
-            )
-            copy.start()
-            copies.append(copy)
-        for copy in copies:
-            copy.wait()
-
-    pl.semaphore_wait(barrier, len(greet))
-
-    def put_rows(at, field, first, second):
-        hs_row[at, 0] = field[first : first + HALF, 0:pcol, :].reshape(HALF * pcol, channels).astype(BF)
-        hs_row[at, 1] = field[second : second + HALF, 0:pcol, :].reshape(HALF * pcol, channels).astype(BF)
-
-    def put_cols(at, field):
-        hs_col[at, 0] = field[:, 0:WIN, :].reshape(prow * WIN, channels).astype(BF)
-        hs_col[at, 1] = field[:, pcol - WIN : pcol, :].reshape(prow * WIN, channels).astype(BF)
-
-    def got_row(at, way):
-        return hr_row[at, way].astype(F32).reshape(HALF, pcol, channels)
-
-    def got_col(at, way):
-        return hr_col[at, way].astype(F32).reshape(prow, WIN, channels)
-
-    put_rows(0, f1, HALF, rows)
-    exchange(0, "row", hs_row, hr_row)
-    f1[0:HALF, 0:pcol, :] = got_row(0, 0)
-    f1[prow - HALF : prow, 0:pcol, :] = got_row(0, 1)
-    put_cols(0, f1)
-    exchange(1, "col", hs_col, hr_col)
-    upper_half = lax.broadcasted_iota(jnp.int32, (prow, WIN, channels), 1) >= HALF
-    f1[:, 0:WIN, :] = jnp.where(upper_half, f1[:, 0:WIN, :], got_col(0, 0))
-    f1[:, pcol - WIN : pcol, :] = jnp.where(
-        upper_half, got_col(0, 1), f1[:, pcol - WIN : pcol, :]
-    )
-
-    @pl.loop(0, n1)
-    def _(j):
-        spots = spots1(j)
-        scatter(h1, spots, attn_forward(gather(f1, spots), 1, n0 + j, usable1(j)))
-
-    @pl.loop(0, rows // strip)
-    def _(j):
-        inner = pl.ds(HALF + j * strip, strip)
-        h = h1[inner, HALF : HALF + cols, :].reshape(flat, channels)
-        g = cot[pl.ds(j * strip, strip)].astype(F32).reshape(flat, channels)
-        result, saved = feed_forward(h, 1)
-        dh = feed_backward(saved, g, 1)
-        out[pl.ds(j * strip, strip)] = result.reshape(strip, cols, channels).astype(BF)
-        dh1[inner, HALF : HALF + cols, :] = dh.reshape(strip, cols, channels)
-
-    @pl.loop(0, n1)
-    def _(j):
-        spots = spots1(j)
-        scatter(g1, spots, attn_backward(gather(dh1, spots), 1, n0 + j))
-
-    put_cols(1, g1)
-    exchange(3, "col", hs_col, hr_col)
-    g1[:, 0:WIN, :] += got_col(1, 0)
-    g1[:, pcol - WIN : pcol, :] += got_col(1, 1)
-    put_rows(1, g1, 0, prow - HALF)
-    exchange(2, "row", hs_row, hr_row)
-    g1[HALF : 2 * HALF, 0:pcol, :] += got_row(1, 0)
-    g1[rows : rows + HALF, 0:pcol, :] += got_row(1, 1)
-
-    @pl.loop(0, rows // strip)
-    def _(j):
-        here = pl.ds(j * strip, strip)
-        g = g1[pl.ds(HALF + j * strip, strip), HALF : HALF + cols, :].reshape(flat, channels)
-        dh = feed_backward((fx[j], fr[j], ff[j], fm[j], fs[j]), g, 0)
-        h0[here] = dh.reshape(strip, cols, channels)
-
-    @pl.loop(0, n0)
-    def _(j):
-        spots = spots0(j)
-        scatter(grad_region, spots, attn_backward(gather(h0, spots), 0, j))
-
-    def stow(unit, x, width):
+    def stow(b, unit, x, width):
         n = x.shape[0] // 16
         for t in range((width + 127) // 128):
             part = x[:, t * 128 : min(width, (t + 1) * 128)]
             wide = part.shape[1]
-            pack[unit + t * n : unit + (t + 1) * n, :, 0:wide] = part.reshape(n, 16, wide).astype(BF)
+            pack[b, unit + t * n : unit + (t + 1) * n, :, 0:wide] = part.reshape(n, 16, wide).astype(BF)
 
     hidden = wup.shape[2]
-    for b in range(2):
-        base = b * U_BLOCK
+    def pack_grads(b):
         for t in range(3):
-            stow(base + U_QKV + 6 * t, a_qkv[b, t], channels)
-        stow(base + U_PROJ, a_proj[b], channels)
-        stow(base + U_UP, a_up[b], hidden)
-        stow(base + U_DOWN, a_down[b], hidden)
+            stow(b, U_QKV + 6 * t, a_qkv[b, t], channels)
+        stow(b, U_PROJ, a_proj[b], channels)
+        stow(b, U_UP, a_up[b], hidden)
+        stow(b, U_DOWN, a_down[b], hidden)
         heads = []
         for h in range(3):
             total = None
@@ -502,85 +417,202 @@
         for t in range(3):
             vec = jnp.where(sub == 5 + t, a_bup[b : b + 1, t * 128 : (t + 1) * 128], vec)
         small = jnp.concatenate([vec] + heads, 0)
-        stow(base + U_SMALL, small, 128)
-
-    source = pack
-    size_now = units
-    at_sem = 0
-    for ph, (size, me, partners) in enumerate(groups):
-        part = size_now // size
+        stow(b, U_SMALL, small, 128)
+
+    def reduce_steps(b):
+        source = pack.at[b]
+        size_now = units
+        at_sem = 0
+        for ph, (size, me, partners) in enumerate(groups):
+            part = size_now // size
+            copies = []
+            for d, neg, member, dev in partners:
+                copy = pltpu.make_async_remote_copy(
+                    src_ref=source.at[pl.ds(member * part, part)],
+                    dst_ref=rs_recv[ph].at[b, neg - 1],
+                    send_sem=red_send.at[b, at_sem + d - 1],
+                    recv_sem=red_recv.at[b, at_sem + neg - 1],
+                    device_id=dev,
+                    device_id_type=MESH,
+                )
+                copy.start()
+                copies.append(copy)
+            yield
+            total = source[pl.ds(me * part, part)].astype(F32)
+            for copy in copies:
+                copy.wait()
+            for d in range(size - 1):
+                total = total + rs_recv[ph][b, d].astype(F32)
+            rs_acc[ph][b] = total.astype(BF)
+            source = rs_acc[ph].at[b]
+            size_now = part
+            at_sem += size - 1
+        for ph in reversed(range(n_ph)):
+            size, me, partners = groups[ph]
+            part = size_now
+            copies = []
+            for d, neg, member, dev in partners:
+                copy = pltpu.make_async_remote_copy(
+                    src_ref=source,
+                    dst_ref=ag_buf[ph].at[b, pl.ds(me * part, part)],
+                    send_sem=red_send.at[b, at_sem + d - 1],
+                    recv_sem=red_recv.at[b, at_sem + neg - 1],
+                    device_id=dev,
+                    device_id_type=MESH,
+                )
+                copy.start()
+                copies.append(copy)
+            ag_buf[ph][b, pl.ds(me * part, part)] = source[...]
+            yield
+            for copy in copies:
+                copy.wait()
+            source = ag_buf[ph].at[b]
+            size_now = part * size
+            at_sem += size - 1
+        (o_low, o_high)[b][...] = source[...]
+
+    for j in range(n0):
+        spots = spots0(j)
+        scatter(h0, spots, attn_forward(gather(f0, spots), 0, j, None))
+
+    for j in range(rows // strip):
+        h = h0[pl.ds(j * strip, strip)].reshape(flat, channels)
+        low, (xhat, rstd, f, m, slope) = feed_forward(h, 0)
+        fx[j], ff[j], fm[j], fs[j] = xhat, f, m, slope
+        fr[j] = jnp.broadcast_to(rstd, xhat.shape)
+        low = low.astype(BF).astype(F32)
+        f1[pl.ds(HALF + j * strip, strip), HALF : HALF + cols, :] = low.reshape(
+            strip, cols, channels
+        )
+
+    def exchange(slot, axis, sends, recvs):
         copies = []
-        for d, neg, member, dev in partners:
+        for way, (step, there) in enumerate(((-1, 1), (1, 0))):
             copy = pltpu.make_async_remote_copy(
-                src_ref=source.at[pl.ds(member * part, part)],
-                dst_ref=rs_recv[ph].at[neg - 1],
-                send_sem=red_send.at[at_sem + d - 1],
-                recv_sem=red_recv.at[at_sem + neg - 1],
-                device_id=dev,
+                src_ref=sends.at[slot // 2, way],
+                dst_ref=recvs.at[slot // 2, there],
+                send_sem=halo_send.at[2 * slot + way],
+                recv_sem=halo_recv.at[2 * slot + there],
+                device_id=side(axis, step),
                 device_id_type=MESH,
             )
             copy.start()
             copies.append(copy)
-        total = source[pl.ds(me * part, part)].astype(F32)
         for copy in copies:
             copy.wait()
-        for d in range(size - 1):
-            total = total + rs_recv[ph][d].astype(F32)
-        rs_acc[ph][...] = total.astype(BF)
-        source = rs_acc[ph]
-        size_now = part
-        at_sem += size - 1
-    for ph in reversed(range(n_ph)):
-        size, me, partners = groups[ph]
-        part = size_now
-        copies = []
-        for d, neg, member, dev in partners:
-            copy = pltpu.make_async_remote_copy(
-                src_ref=source,
-                dst_ref=ag_buf[ph].at[pl.ds(me * part, part)],
-                send_sem=red_send.at[at_sem + d - 1],
-                recv_sem=red_recv.at[at_sem + neg - 1],
-                device_id=dev,
-                device_id_type=MESH,
-            )
-            copy.start()
-            copies.append(copy)
-        ag_buf[ph][pl.ds(me * part, part)] = source[...]
-        for copy in copies:
-            copy.wait()
-        source = ag_buf[ph]
-        size_now = part * size
-        at_sem += size - 1
-
-    def fetch(unit, n, width=128):
-        return source[unit : unit + n].astype(F32).reshape(n * 16, 128)[:, :width]
-
-    for b in range(2):
-        base = b * U_BLOCK
+
+    pl.semaphore_wait(barrier, len(greet))
+
+    def put_rows(at, field, first, second):
+        hs_row[at, 0] = field[first : first + HALF, 0:pcol, :].reshape(HALF * pcol, channels).astype(BF)
+        hs_row[at, 1] = field[second : second + HALF, 0:pcol, :].reshape(HALF * pcol, channels).astype(BF)
+
+    def put_cols(at, field):
+        hs_col[at, 0] = field[:, 0:WIN, :].reshape(prow * WIN, channels).astype(BF)
+        hs_col[at, 1] = field[:, pcol - WIN : pcol, :].reshape(prow * WIN, channels).astype(BF)
+
+    def got_row(at, way):
+        return hr_row[at, way].astype(F32).reshape(HALF, pcol, channels)
+
+    def got_col(at, way):
+        return hr_col[at, way].astype(F32).reshape(prow, WIN, channels)
+
+    put_rows(0, f1, HALF, rows)
+    exchange(0, "row", hs_row, hr_row)
+    f1[0:HALF, 0:pcol, :] = got_row(0, 0)
+    f1[prow - HALF : prow, 0:pcol, :] = got_row(0, 1)
+    put_cols(0, f1)
+    exchange(1, "col", hs_col, hr_col)
+    upper_half = lax.broadcasted_iota(jnp.int32, (prow, WIN, channels), 1) >= HALF
+    f1[:, 0:WIN, :] = jnp.where(upper_half, f1[:, 0:WIN, :], got_col(0, 0))
+    f1[:, pcol - WIN : pcol, :] = jnp.where(
+        upper_half, got_col(0, 1), f1[:, pcol - WIN : pcol, :]
+    )
+
+    for j in range(n1):
+        spots = spots1(j)
+        scatter(h1, spots, attn_forward(gather(f1, spots), 1, n0 + j, usable1(j)))
+
+    for j in range(rows // strip):
+        inner = pl.ds(HALF + j * strip, strip)
+        h = h1[inner, HALF : HALF + cols, :].reshape(flat, channels)
+        g = cot[pl.ds(j * strip, strip)].astype(F32).reshape(flat, channels)
+        result, saved = feed_forward(h, 1)
+        dh = feed_backward(saved, g, 1)
+        out[pl.ds(j * strip, strip)] = result.reshape(strip, cols, channels).astype(BF)
+        dh1[inner, HALF : HALF + cols, :] = dh.reshape(strip, cols, channels)
+
+    for j in range(n1):
+        spots = spots1(j)
+        scatter(g1, spots, attn_backward(gather(dh1, spots), 1, n0 + j))
+
+    pack_grads(1)
+    high = reduce_steps(1)
+    next(high, None)
+    put_cols(1, g1)
+    exchange(3, "col", hs_col, hr_col)
+    g1[:, 0:WIN, :] += got_col(1, 0)
+    g1[:, pcol - WIN : pcol, :] += got_col(1, 1)
+    next(high, None)
+    put_rows(1, g1, 0, prow - HALF)
+    exchange(2, "row", hs_row, hr_row)
+    g1[HALF : 2 * HALF, 0:pcol, :] += got_row(1, 0)
+    g1[rows : rows + HALF, 0:pcol, :] += got_row(1, 1)
+    next(high, None)
+
+    for j in range(rows // strip):
+        here = pl.ds(j * strip, strip)
+        g = g1[pl.ds(HALF + j * strip, strip), HALF : HALF + cols, :].reshape(flat, channels)
+        dh = feed_backward((fx[j], fr[j], ff[j], fm[j], fs[j]), g, 0)
+        h0[here] = dh.reshape(strip, cols, channels)
+        if j % 2:
+            next(high, None)
+
+    for j in range(n0):
+        spots = spots0(j)
+        scatter(grad_region, spots, attn_backward(gather(h0, spots), 0, j))
+        next(high, None)
+
+    pack_grads(0)
+    low = reduce_steps(0)
+    next(low, None)
+    for _ in high:
+        pass
+    for _ in low:
+        pass
+
+def finish(
+    out, grad_region, low, high, o_out, o_region, o_gains, o_qkv, o_qkv_bias, o_table, o_proj, o_up, o_up_bias, o_down
+):
+    channels = out.shape[2]
+    o_out[...] = out[...]
+    o_region[...] = grad_region[...]
+    hots = [offsets(c) for c in range(WIN)]
+    for b, source in enumerate((low, high)):
+
+        def fetch(unit, n, width=128):
+            return source[unit : unit + n].astype(F32).reshape(n * 16, 128)[:, :width]
+
+        o_qkv[b] = jnp.concatenate([fetch(U_QKV + 6 * t, 6, channels) for t in range(3)], 1)
         for t in range(3):
-            o_qkv[b, t] = fetch(base + U_QKV + 6 * t, 6, channels)
-            o_up[b, :, t * 128 : (t + 1) * 128] = fetch(base + U_UP + 6 * t, 6)
-            o_down[b, :, t * 128 : (t + 1) * 128] = fetch(base + U_DOWN + 6 * t, 6)
-        o_proj[b] = fetch(base + U_PROJ, 6, channels)
-        o_small[b] = fetch(base + U_SMALL, 2)
-
-
-def expand_table(table):
-    side = 2 * WIN - 1
-    grid = table.reshape(2, -1, side, side)
-    x = jnp.stack([grid[..., WIN - 1 - c : side - c] for c in range(WIN)], 2)
-    return x.reshape(2, grid.shape[1], WIN, side * WIN)
-
-
-def fold_table(dx):
-    side = 2 * WIN - 1
-    x = dx.reshape(2, -1, WIN, side, WIN)
-    total = 0.0
-    for c in range(WIN):
-        total = total + jnp.pad(
-            x[:, :, c], ((0, 0), (0, 0), (0, 0), (WIN - 1 - c, c))
-        )
-    return total.reshape(2, -1, side * side)
+            o_up[b, :, t * 128 : (t + 1) * 128] = fetch(U_UP + 6 * t, 6)
+            o_down[b, :, t * 128 : (t + 1) * 128] = fetch(U_DOWN + 6 * t, 6)
+        o_proj[b] = fetch(U_PROJ, 6, channels)
+        small = fetch(U_SMALL, 2)
+        o_gains[b] = small[3:5, :channels]
+        o_qkv_bias[b : b + 1, :] = jnp.concatenate([small[t : t + 1, :channels] for t in range(3)], 1)
+        for t in range(3):
+            o_up_bias[b : b + 1, t * 128 : (t + 1) * 128] = small[5 + t : 6 + t]
+        tables = small[8:32]
+        row = lax.rem(lax.broadcasted_iota(jnp.int32, tables.shape, 0), WIN)
+        lane = lax.broadcasted_iota(jnp.int32, tables.shape, 1)
+        total = None
+        for c in range(WIN):
+            mine = jnp.where((row == c) & (lane < (2 * WIN - 1) * WIN), tables, 0.0)
+            term = dot_nt(mine.astype(BF), hots[c])
+            total = term if total is None else total + term
+        for h in range(3):
+            o_table[b, h : h + 1, :] = jnp.sum(total[h * WIN : (h + 1) * WIN], 0, keepdims=True)
 
 
 def body(n_row, n_col, region, cotangent, gains, wqkv, bqkv, table, wproj, wup, bup, wdown):
@@ -588,7 +620,7 @@
     hidden = wup.shape[2]
     prow, pcol = rows + WIN, cols + WIN
     devices = n_row * n_col
-    units = -(-2 * U_BLOCK // devices) * devices
+    units = -(-U_BLOCK // devices) * devices
     phases = factors(n_row, n_col)
     sizes = []
     for phase in phases:
@@ -599,21 +631,18 @@
     recv, acc, gath = [], [], []
     now = units
     for size in sizes:
-        gath.append(pltpu.VMEM((now, 16, 128), BF))
+        gath.append(pltpu.VMEM((2, now, 16, 128), BF))
         now //= size
-        recv.append(pltpu.VMEM((size - 1, now, 16, 128), BF))
-        acc.append(pltpu.VMEM((now, 16, 128), BF))
+        recv.append(pltpu.VMEM((2, size - 1, now, 16, 128), BF))
+        acc.append(pltpu.VMEM((2, now, 16, 128), BF))
     turns = cols // (3 * WIN) + (pcol + WIN) // (2 * WIN)
     steps = 2 * sum(s - 1 for s in sizes)
     vmem = pl.BlockSpec(memory_space=pltpu.VMEM)
     shapes = [
         jax.ShapeDtypeStruct((rows, cols, channels), BF),
         jax.ShapeDtypeStruct((rows, cols, channels), F32),
-        jax.ShapeDtypeStruct((2, 3, channels, channels), F32),
-        jax.ShapeDtypeStruct((2, channels, channels), F32),
-        jax.ShapeDtypeStruct((2, channels, hidden), F32),
-        jax.ShapeDtypeStruct((2, channels, hidden), F32),
-        jax.ShapeDtypeStruct((2, 32, 128), F32),
+        jax.ShapeDtypeStruct((units, 16, 128), BF),
+        jax.ShapeDtypeStruct((units, 16, 128), BF),
     ]
     field0 = pltpu.VMEM((rows, cols, channels), F32)
     field1 = pltpu.VMEM((prow, pcol + WIN, channels), F32)
@@ -624,6 +653,7 @@
         out_specs=[vmem] * len(shapes),
         scratch_shapes=[
             pltpu.VMEM((2, 3, channels, channels), BF),
+            pltpu.VMEM((2, 3, WIN, 128), F32),
             pltpu.VMEM((2, 3 * TOK, 2 * TOK), F32),
             field0,
             field0,
@@ -644,7 +674,7 @@
             pltpu.VMEM((2, 2, prow * WIN, channels), BF),
             pltpu.SemaphoreType.DMA((8,)),
             pltpu.SemaphoreType.DMA((8,)),
-            pltpu.VMEM((units, 16, 128), BF),
+            pltpu.VMEM((2, units, 16, 128), BF),
             *[pltpu.VMEM((turns, GROUP * TOK, channels), BF)] * 3,
             pltpu.VMEM((turns, GROUP // 2, 3 * TOK, 2 * TOK), F32),
             *[pltpu.VMEM((turns, GROUP * TOK, channels), BF)] * 2,
@@ -656,28 +686,34 @@
             *recv,
             *acc,
             *gath,
-            pltpu.SemaphoreType.DMA((steps,)),
-            pltpu.SemaphoreType.DMA((steps,)),
+            pltpu.SemaphoreType.DMA((2, steps)),
+            pltpu.SemaphoreType.DMA((2, steps)),
         ],
         compiler_params=pltpu.CompilerParams(
             collective_id=0, has_side_effects=True, vmem_limit_bytes=48 * 1024 * 1024
         ),
         name="swin_pair",
-    )(region, cotangent, gains, wqkv, bqkv, expand_table(table), wproj, wup, bup, wdown.transpose(0, 2, 1))
-    out, grad_region, dqkv, dproj, dup, down_t, small = results
-    vec = small[:, 0:5, :channels]
-    return (
-        out,
-        grad_region,
-        vec[:, 3:5],
-        dqkv.transpose(0, 2, 1, 3).reshape(2, channels, 3 * channels),
-        vec[:, 0:3].reshape(2, 3 * channels),
-        fold_table(small[:, 8:32, : (2 * WIN - 1) * WIN].reshape(2, 3, WIN, -1)),
-        dproj,
-        dup,
-        small[:, 5:8].reshape(2, hidden),
-        down_t.transpose(0, 2, 1),
-    )
+    )(region, cotangent, gains, wqkv, bqkv, table, wproj, wup, bup, wdown.transpose(0, 2, 1))
+    finals = [
+        *shapes[:2],
+        jax.ShapeDtypeStruct((2, 2, channels), F32),
+        jax.ShapeDtypeStruct((2, channels, 3 * channels), F32),
+        jax.ShapeDtypeStruct((2, 3 * channels), F32),
+        jax.ShapeDtypeStruct(table.shape, F32),
+        jax.ShapeDtypeStruct((2, channels, channels), F32),
+        jax.ShapeDtypeStruct((2, channels, hidden), F32),
+        jax.ShapeDtypeStruct((2, hidden), F32),
+        jax.ShapeDtypeStruct((2, channels, hidden), F32),
+    ]
+    results = pl.pallas_call(
+        finish,
+        out_shape=finals,
+        in_specs=[vmem] * 4,
+        out_specs=[vmem] * len(finals),
+        compiler_params=pltpu.CompilerParams(vmem_limit_bytes=32 * 1024 * 1024),
+        name="finish",
+    )(*results)
+    return (*results[:9], results[9].transpose(0, 2, 1))
 
 
 def solution(mesh):

time: 76 us -> 76.4 us (level)
  Pallas kernels: 65.1 us -> 68.7 us
  local copies, waits for them, and re-layouts: 9.7 us -> 6.7 us
    reshape x4 -> x0, local copies, waits for them, and re-layouts: 2.13 us -> none  [the longest x1 0.78 us: expand_table(): grid = table.reshape(2, -1, side, side)]
    pallas_call x1, Pallas kernels: 65.1 us -> 67 us  [body(): pl.pallas_call(functools.partial(kernel, n_row, n_col, units), out_shape=...]
    pallas_call x0 -> x1, Pallas kernels: none -> 1.77 us  [body(): pl.pallas_call(finish, out_shape=finals, in_specs=[vmem] * 4, out_specs=[...]
    unnamed x26 -> x20, local copies, waits for them, and re-layouts: 5.61 us -> 6.7 us
    another operation x18 -> x0, local copies, waits for them, and re-layouts: 1.06 us -> none  [the longest x17 0.85 us: expand_table(): x = jnp.stack([grid[..., WIN - 1 - c:side - c] for c in range(WIN)], 2)]
where the time goes in v3:
time: 76.4 us; the launch traced here: 76.1 us
  Pallas kernels  68.7 us (90%)
  local copies, waits for them, and re-layouts  6.7 us (9%)
    pallas_call x1, Pallas kernels, body(): pl.pallas_call(functools.partial(kernel, n_row, n_col, units), out_shape=...  67 us
    unnamed x20, local copies, waits for them, and re-layouts  6.7 us
    pallas_call x1, Pallas kernels, body(): pl.pallas_call(finish, out_shape=finals, in_specs=[vmem] * 4, out_specs=[...  1.77 us

profile of v3, /device:TPU:0, one launch (start us, length us, event | category | flops | bytes accessed | tf_op | source)
XLA Modules:
  0.0 76.1 jit_solution(1231610431421455906)
XLA Ops:
  0.6 0.0 copy-start.6
  0.7 0.0 copy-start.7
  0.7 0.0 copy-start.8
  0.7 0.7 copy.20.table
  1.4 0.0 copy-done.6
  1.4 0.0 copy-done.7
  1.4 0.0 copy-done.8
  1.4 0.0 copy-start
  1.4 0.9 %copy-done = bf16[16,48,96]{2,1,0:T(8,128)(2,1)S(1)} copy-done((bf16[16,48,96]{2,1,0:T(8,128)(2,1)S(1)}, bf16[16,48,96]{2,1,0:T(8,128)(2,1)}, u32[]{:S(2)}) %copy-start) | copy-done | bytes 147480
  2.3 0.0 copy-start.1
  2.3 0.9 %copy-done.1 = bf16[16,48,96]{2,1,0:T(8,128)(2,1)S(1)} copy-done((bf16[16,48,96]{2,1,0:T(8,128)(2,1)S(1)}, bf16[16,48,96]{2,1,0:T(8,128)(2,1)}, u32[]{:S(2)}) %copy-start.1) | copy-done | bytes 147480
  3.3 0.0 copy-start.2
  3.3 0.9 %copy-done.2 = bf16[2,96,288]{2,1,0:T(8,128)(2,1)S(1)} copy-done((bf16[2,96,288]{2,1,0:T(8,128)(2,1)S(1)}, bf16[2,96,288]{2,1,0:T(8,128)(2,1)}, u32[]{:S(2)}) %copy-start.2) | copy-done | bytes 110616
  4.2 0.0 copy-start.3
  4.2 0.9 %copy-done.3 = bf16[2,96,384]{2,1,0:T(8,128)(2,1)S(1)} copy-done((bf16[2,96,384]{2,1,0:T(8,128)(2,1)S(1)}, bf16[2,96,384]{2,1,0:T(8,128)(2,1)}, u32[]{:S(2)}) %copy-start.3) | copy-done | bytes 147480
  5.1 0.0 copy-start.4
  5.1 0.9 %copy-done.4 = bf16[2,384,96]{1,2,0:T(8,128)(2,1)S(1)} copy-done((bf16[2,384,96]{1,2,0:T(8,128)(2,1)S(1)}, bf16[2,384,96]{1,2,0:T(8,128)(2,1)}, u32[]{:S(2)}) %copy-start.4) | copy-done | bytes 147480
  6.0 0.0 copy-start.5
  6.0 0.8 %copy-done.5 = bf16[2,96,96]{2,1,0:T(8,128)(2,1)S(1)} copy-done((bf16[2,96,96]{2,1,0:T(8,128)(2,1)S(1)}, bf16[2,96,96]{2,1,0:T(8,128)(2,1)}, u32[]{:S(2)}) %copy-start.5) | copy-done | bytes 36888
  6.8 67.0 %swin_pair.1 = (bf16[16,48,96]{2,1,0:T(8,128)(2,1)S(1)}, f32[16,48,96]{2,1,0:T(8,128)S(1)}, bf16[64,16,128]{2,1,0:T(8,128)(2,1)S(1)}, bf16[64,16,128]{2,1,0:T(8,128)(2,1)S(1)}) custom-call(bf16[16,48,96]{2,1,0:T(8,128)(2,1)S(1)} %copy-done, bf16[16,48,96]{2,1,0:T(8,128)(2,1)S(1)} %copy-done.1, f32[2,2,96]{2,1,0:T(2,128)S(1)} %copy-done.8, ...), custom_call_target="tpu_custom_call" | custom-call | tf_op jit(solution)/shard_map/swin_pair/pallas_call | solution.py:649
  73.8 1.8 %finish.1 = (bf16[16,48,96]{2,1,0:T(8,128)(2,1)}, f32[16,48,96]{2,1,0:T(8,128)}, f32[2,2,96]{2,1,0:T(2,128)}, f32[2,96,288]{2,1,0:T(8,128)}, f32[2,288]{1,0:T(2,...) custom-call(bf16[16,48,96]{2,1,0:T(8,128)(2,1)S(1)} %get-tuple-eleme, ...), custom_call_target="tpu_custom_call" | custom-call | tf_op jit(solution)/shard_map/finish/pallas_call | solution.py:708
  75.5 0.6 copy.21
Async XLA Ops:
  0.6 0.7 copy-start.6
  0.7 0.7 copy-start.7
  0.7 0.7 copy-start.8
  1.4 0.9 %copy-start = (bf16[16,48,96]{2,1,0:T(8,128)(2,1)S(1)}, bf16[16,48,96]{2,1,0:T(8,128)(2,1)}, u32[]{:S(2)}) copy-start(bf16[16,48,96]{2,1,0:T(8,128)(2,1)} %region.1) | copy-start | bytes 442372
  2.3 0.9 %copy-start.1 = (bf16[16,48,96]{2,1,0:T(8,128)(2,1)S(1)}, bf16[16,48,96]{2,1,0:T(8,128)(2,1)}, u32[]{:S(2)}) copy-start(bf16[16,48,96]{2,1,0:T(8,128)(2,1)} %cot.1) | copy-start | bytes 442372
  3.3 0.9 %copy-start.2 = (bf16[2,96,288]{2,1,0:T(8,128)(2,1)S(1)}, bf16[2,96,288]{2,1,0:T(8,128)(2,1)}, u32[]{:S(2)}) copy-start(bf16[2,96,288]{2,1,0:T(8,128)(2,1)} %wqkv.1) | copy-start | bytes 331780
  4.2 0.9 %copy-start.3 = (bf16[2,96,384]{2,1,0:T(8,128)(2,1)S(1)}, bf16[2,96,384]{2,1,0:T(8,128)(2,1)}, u32[]{:S(2)}) copy-start(bf16[2,96,384]{2,1,0:T(8,128)(2,1)} %wup.1) | copy-start | bytes 442372
  5.1 0.9 %copy-start.4 = (bf16[2,384,96]{1,2,0:T(8,128)(2,1)S(1)}, bf16[2,384,96]{1,2,0:T(8,128)(2,1)}, u32[]{:S(2)}) copy-start(bf16[2,384,96]{1,2,0:T(8,128)(2,1)} %param.19) | copy-start | bytes 442372
  6.0 0.8 %copy-start.5 = (bf16[2,96,96]{2,1,0:T(8,128)(2,1)S(1)}, bf16[2,96,96]{2,1,0:T(8,128)(2,1)}, u32[]{:S(2)}) copy-start(bf16[2,96,96]{2,1,0:T(8,128)(2,1)} %wproj.1) | copy-start | bytes 110596

commit v4 on v3

--- a/solution.py
+++ b/solution.py
@@ -346,14 +346,14 @@
 
     def spots0(j):
         return [
-            (i * WIN, (j * 3 + c) * WIN)
+            (i * WIN, pl.multiple_of((j * 3 + c) * WIN, WIN))
             for i in range(rows // WIN)
             for c in range(3)
         ]
 
     def spots1(j):
         return [
-            (i * WIN, (j * 2 + c) * WIN)
+            (i * WIN, pl.multiple_of((j * 2 + c) * WIN, WIN))
             for i in range(prow // WIN)
             for c in range(2)
         ]
@@ -471,11 +471,13 @@
             at_sem += size - 1
         (o_low, o_high)[b][...] = source[...]
 
-    for j in range(n0):
+    @pl.loop(0, n0)
+    def _(j):
         spots = spots0(j)
         scatter(h0, spots, attn_forward(gather(f0, spots), 0, j, None))
 
-    for j in range(rows // strip):
+    @pl.loop(0, rows // strip)
+    def _(j):
         h = h0[pl.ds(j * strip, strip)].reshape(flat, channels)
         low, (xhat, rstd, f, m, slope) = feed_forward(h, 0)
         fx[j], ff[j], fm[j], fs[j] = xhat, f, m, slope
@@ -529,11 +531,13 @@
         upper_half, got_col(0, 1), f1[:, pcol - WIN : pcol, :]
     )
 
-    for j in range(n1):
+    @pl.loop(0, n1)
+    def _(j):
         spots = spots1(j)
         scatter(h1, spots, attn_forward(gather(f1, spots), 1, n0 + j, usable1(j)))
 
-    for j in range(rows // strip):
+    @pl.loop(0, rows // strip)
+    def _(j):
         inner = pl.ds(HALF + j * strip, strip)
         h = h1[inner, HALF : HALF + cols, :].reshape(flat, channels)
         g = cot[pl.ds(j * strip, strip)].astype(F32).reshape(flat, channels)
@@ -542,7 +546,8 @@
         out[pl.ds(j * strip, strip)] = result.reshape(strip, cols, channels).astype(BF)
         dh1[inner, HALF : HALF + cols, :] = dh.reshape(strip, cols, channels)
 
-    for j in range(n1):
+    @pl.loop(0, n1)
+    def _(j):
         spots = spots1(j)
         scatter(g1, spots, attn_backward(gather(dh1, spots), 1, n0 + j))
 
@@ -560,25 +565,27 @@
     g1[rows : rows + HALF, 0:pcol, :] += got_row(1, 1)
     next(high, None)
 
-    for j in range(rows // strip):
+    @pl.loop(0, rows // strip)
+    def _(j):
         here = pl.ds(j * strip, strip)
         g = g1[pl.ds(HALF + j * strip, strip), HALF : HALF + cols, :].reshape(flat, channels)
         dh = feed_backward((fx[j], fr[j], ff[j], fm[j], fs[j]), g, 0)
         h0[here] = dh.reshape(strip, cols, channels)
-        if j % 2:
-            next(high, None)
-
-    for j in range(n0):
+
+    next(high, None)
+
+    @pl.loop(0, n0)
+    def _(j):
         spots = spots0(j)
         scatter(grad_region, spots, attn_backward(gather(h0, spots), 0, j))
-        next(high, None)
+
+    next(high, None)
 
     pack_grads(0)
     low = reduce_steps(0)
-    next(low, None)
+    for _ in low:
+        next(high, None)
     for _ in high:
-        pass
-    for _ in low:
         pass
 
 def finish(
@@ -690,7 +697,7 @@
             pltpu.SemaphoreType.DMA((2, steps)),
         ],
         compiler_params=pltpu.CompilerParams(
-            collective_id=0, has_side_effects=True, vmem_limit_bytes=48 * 1024 * 1024
+            collective_id=0, has_side_effects=True, vmem_limit_bytes=60 * 1024 * 1024
         ),
         name="swin_pair",
     )(region, cotangent, gains, wqkv, bqkv, table, wproj, wup, bup, wdown.transpose(0, 2, 1))

time: 76.4 us -> 79.9 us (1.046)
  Pallas kernels: 68.7 us -> 73.3 us
  local copies, waits for them, and re-layouts: 6.7 us -> 5.7 us
    pallas_call x1, Pallas kernels: 67 us -> 71.5 us  [body(): pl.pallas_call(functools.partial(kernel, n_row, n_col, units), out_shape=...]
    unnamed x20 -> x10, local copies, waits for them, and re-layouts: 6.7 us -> 5.7 us
where the time goes in v4:
time: 79.9 us; the launch traced here: 79.6 us
  Pallas kernels  73.3 us (92%)
  local copies, waits for them, and re-layouts  5.7 us (7%)
    pallas_call x1, Pallas kernels, body(): pl.pallas_call(functools.partial(kernel, n_row, n_col, units), out_shape=...  71.5 us
    unnamed x10, local copies, waits for them, and re-layouts  5.7 us
    pallas_call x1, Pallas kernels, body(): pl.pallas_call(finish, out_shape=finals, in_specs=[vmem] * 4, out_specs=[...  1.77 us

profile of v4, /device:TPU:0, one launch (start us, length us, event | category | flops | bytes accessed | tf_op | source)
XLA Modules:
  0.0 79.6 jit_solution(916346014022674404)
XLA Ops:
  0.6 1.3 %copy.20.table = f32[2,3,225]{2,1,0:T(4,128)} copy(f32[2,3,225]{2,0,1:T(2,128)} %param.15) | data formatting | bytes 10800 | tf_op args[5]
  1.9 71.5 %swin_pair.1 = (bf16[16,48,96]{2,1,0:T(8,128)(2,1)}, f32[16,48,96]{2,1,0:T(8,128)}, bf16[64,16,128]{2,1,0:T(8,128)(2,1)}, bf16[64,16,128]{2,1,0:T(8,128)(2,1)}) custom-call(bf16[16,48,96]{2,1,0:T(8,128)(2,1)} %region.1, bf16[16,48,96]{2,1,0:T(8,128)(2,1)} %cot.1, f32[2,2,96]{2,1,0:T(2,128)} %gains.1, bf16[2,96,288]{2,1,0:T(8,128)(2,1)} %wqkv.1, ...), custom_call_target="tpu_custom_call" | custom-call | tf_op jit(solution)/shard_map/swin_pair/pallas_call | solution.py:656
  73.5 0.0 copy-start
  73.5 1.0 %copy-done = f32[16,48,96]{2,1,0:T(8,128)S(1)} copy-done((f32[16,48,96]{2,1,0:T(8,128)S(1)}, f32[16,48,96]{2,1,0:T(8,128)}, u32[]{:S(2)}) %copy-start) | copy-done | bytes 294936
  74.4 0.0 copy-start.1
  74.5 0.9 %copy-done.1 = bf16[64,16,128]{2,1,0:T(8,128)(2,1)S(1)} copy-done((bf16[64,16,128]{2,1,0:T(8,128)(2,1)S(1)}, bf16[64,16,128]{2,1,0:T(8,128)(2,1)}, u32[]{:S(2)}) %copy-start.1) | copy-done | bytes 262168
  75.4 0.0 copy-start.2
  75.4 0.9 %copy-done.2 = bf16[64,16,128]{2,1,0:T(8,128)(2,1)S(1)} copy-done((bf16[64,16,128]{2,1,0:T(8,128)(2,1)S(1)}, bf16[64,16,128]{2,1,0:T(8,128)(2,1)}, u32[]{:S(2)}) %copy-start.2) | copy-done | bytes 262168
  76.4 0.0 copy-start.3
  76.4 0.9 %copy-done.3 = bf16[16,48,96]{2,1,0:T(8,128)(2,1)S(1)} copy-done((bf16[16,48,96]{2,1,0:T(8,128)(2,1)S(1)}, bf16[16,48,96]{2,1,0:T(8,128)(2,1)}, u32[]{:S(2)}) %copy-start.3) | copy-done | bytes 147480
  77.3 1.8 %finish.1 = (bf16[16,48,96]{2,1,0:T(8,128)(2,1)}, f32[16,48,96]{2,1,0:T(8,128)}, f32[2,2,96]{2,1,0:T(2,128)}, f32[2,96,288]{2,1,0:T(8,128)}, f32[2,288]{1,0:T(2,...) custom-call(bf16[16,48,96]{2,1,0:T(8,128)(2,1)S(1)} %copy-done.3, ...), custom_call_target="tpu_custom_call" | custom-call | tf_op jit(solution)/shard_map/finish/pallas_call | solution.py:715
  79.0 0.6 copy.21
Async XLA Ops:
  73.5 1.0 %copy-start = (f32[16,48,96]{2,1,0:T(8,128)S(1)}, f32[16,48,96]{2,1,0:T(8,128)}, u32[]{:S(2)}) copy-start(f32[16,48,96]{2,1,0:T(8,128)} %get-tuple-element.25.grad_region) | copy-start | bytes 884740
  74.4 0.9 %copy-start.1 = (bf16[64,16,128]{2,1,0:T(8,128)(2,1)S(1)}, bf16[64,16,128]{2,1,0:T(8,128)(2,1)}, u32[]{:S(2)}) copy-start(bf16[64,16,128]{2,1,0:T(8,128)(2,1)} %get-tuple-element.26.low) | copy-start | bytes 786436
  75.4 0.9 %copy-start.2 = (bf16[64,16,128]{2,1,0:T(8,128)(2,1)S(1)}, bf16[64,16,128]{2,1,0:T(8,128)(2,1)}, u32[]{:S(2)}) copy-start(bf16[64,16,128]{2,1,0:T(8,128)(2,1)} %get-tuple-element.27.high) | copy-start | bytes 786436
  76.4 0.9 %copy-start.3 = (bf16[16,48,96]{2,1,0:T(8,128)(2,1)S(1)}, bf16[16,48,96]{2,1,0:T(8,128)(2,1)}, u32[]{:S(2)}) copy-start(bf16[16,48,96]{2,1,0:T(8,128)(2,1)} %get-tuple-element.24.out) | copy-start | bytes 442372
